TPU v7x, 128 devices: a whole 4x4x4 slice. The times are simulated.
128 devices in a mesh: night: 4 (over z), bl: 32 (over y, x, core).
Axes of the slice: x: 4, y: 4, z: 4, core: 2. Of those that a mesh axis runs over, the one named last changes fastest.
Arguments:
- visibilities: float32 [2, 4, 128, 30, 768], P(None, 'night', 'bl'), may hold values from -6 to 6
- corrupted_sample_markers: int32 [4, 768], P('night'), may hold values from 0 to 1073741823
- antenna_gain_table: float32 [2, 4, 352, 768], P(None, 'night', 'bl'), may hold values from -4 to 4
- baseline_antennas: int32 [128, 2], P('bl'), may hold values from 0 to 351
- first_bin: int32 [4], P('night'), may hold values from 0 to 96
- tap_offsets: int32 [4, 32], P('night'), may hold values from 0 to 26
- tap_weights: float32 [4, 32, 4], P('night'), may hold values from 0.1 to 0.5
- lst_delay: float32 [4, 32], P('night'), may hold values from -1 to 1
- fringe_rate: float32 [128], P('bl'), may hold values from -3 to 3
Outputs:
- binned: float32 [2, 128, 128, 768], P(None, ('night', 'bl'))
- weight_total: float32 [128, 768], P(('night', 'bl'))
All inputs are finite; a program needn't handle non-finite values.
Results may differ from a plain program's by a relative error of at most 0.0001.
Values sent between devices are 32-bit elements; how exact they have to be, the bound alone decides.
A program may use at most 64 MiB of HBM per device.

v0:
```python
import jax
import jax.numpy as jnp
from jax import lax
from jax.sharding import PartitionSpec as P

LB_DEV = 1


finest_accuracy = lax.Precision.HIGHEST


def unpack_reject_markers(packed, sample_indices):
    sample = jnp.arange(sample_indices, dtype=jnp.int32)
    flag_bits = jnp.bitwise_and(jnp.right_shift(packed[..., None, :], sample[:, None]), 1)
    return 1.0 - flag_bits.astype(jnp.float32)


def tap_matrix(offsets, weights, sample_indices):
    sample = jnp.arange(sample_indices, dtype=jnp.int32)
    tap_index = jnp.arange(weights.shape[-1], dtype=jnp.int32)
    matches = sample == offsets[..., None, None] + tap_index[:, None]
    return jnp.sum(jnp.where(matches, weights[..., None], jnp.float32(0.0)), axis=-2)


def per_device(
    visibilities,
    corrupted_sample_markers,
    antenna_gain_table,
    baseline_antennas,
    first_bin,
    tap_offsets,
    tap_weights,
    lst_delay,
    fringe_rate,
):
    night_count = lax.axis_size("night")
    block_count = lax.axis_size("bl")
    block_rows = visibilities.shape[2]
    sample_indices = visibilities.shape[3]
    channels = visibilities.shape[4]
    bin_count = tap_offsets.shape[1]
    all_bins = LB_DEV * night_count * block_count
    compressed_reject_integers, offsets_all, first_all = (
        lax.all_gather(corrupted_sample_markers, "night", axis=0, tiled=True),
        lax.all_gather(tap_offsets, "night", axis=0, tiled=True),
        lax.all_gather(first_bin, "night", axis=0, tiled=True),
    )
    weights_all = lax.all_gather(tap_weights, "night", axis=0, tiled=True)
    gains_all = lax.all_gather(antenna_gain_table, "bl", axis=2, tiled=True)
    clean_sample_selector = unpack_reject_markers(compressed_reject_integers, sample_indices)
    interpolant_kernels = tap_matrix(offsets_all, weights_all, sample_indices)
    evening_share = jnp.einsum(
        "bdr,bro->bdo", interpolant_kernels, clean_sample_selector, precision=finest_accuracy
    )
    evening_slot = lax.axis_index("night")
    own_matrix = lax.dynamic_index_in_dim(interpolant_kernels, evening_slot, 0, keepdims=False)
    retained_selector = lax.dynamic_index_in_dim(
        clean_sample_selector, evening_slot, 0, keepdims=False
    )[None]
    first_gain = jnp.take(gains_all[:, 0], baseline_antennas[:, 0], axis=1)
    second_gain = jnp.take(gains_all[:, 0], baseline_antennas[:, 1], axis=1)
    gain_re = (first_gain[0] * second_gain[0] + first_gain[1] * second_gain[1])[:, None, :]
    gain_im = (first_gain[1] * second_gain[0] - first_gain[0] * second_gain[1])[:, None, :]
    real_part = visibilities[0, 0]
    imag_part = visibilities[1, 0]
    calibrated = jnp.stack(
        [
            (gain_re * real_part - gain_im * imag_part) * retained_selector,
            (gain_re * imag_part + gain_im * real_part) * retained_selector,
        ]
    )
    binned_night = jnp.einsum("lt,xbtc->xlbc", own_matrix, calibrated, precision=finest_accuracy)
    frequency = 1.0 + jnp.arange(channels, dtype=jnp.float32) / channels
    angle = fringe_rate[None, :, None] * lst_delay[0][:, None, None] * frequency[None, None, :]
    cosine = jnp.cos(angle)
    sine_part = jnp.sin(angle)
    rotated = jnp.stack(
        [
            cosine * binned_night[0] - sine_part * binned_night[1],
            sine_part * binned_night[0] + cosine * binned_night[1],
        ]
    )
    anchor = jnp.zeros((), jnp.int32)
    bin_grid = jnp.zeros((2, all_bins, block_rows, channels), jnp.float32)
    bin_grid = lax.dynamic_update_slice(bin_grid, rotated, (anchor, first_bin[0], anchor, anchor))
    sources = night_count * block_count
    arrived = lax.all_to_all(
        bin_grid.reshape(2, sources, LB_DEV, block_rows, channels),
        ("night", "bl"),
        split_axis=1,
        concat_axis=3,
        tiled=True,
    )
    summed = jnp.sum(
        arrived.reshape(2, LB_DEV, night_count, block_count * block_rows, channels), axis=2
    )
    row_first = (evening_slot * block_count + lax.axis_index("bl")) * LB_DEV
    bin_rows = row_first + jnp.arange(LB_DEV, dtype=jnp.int32)
    position = bin_rows[None, :] - first_all[:, None]
    select = (position[:, :, None] == jnp.arange(bin_count, dtype=jnp.int32)[None, None, :]).astype(
        jnp.float32
    )
    weight_total = jnp.einsum("nil,nlc->ic", select, evening_share, precision=finest_accuracy)
    binned = summed / jnp.maximum(weight_total, 0.5)[None, :, None, :]
    return (binned, weight_total)


def solution(mesh):
    placed = (
        P(None, "night", "bl", None, None),
        P("night", None),
        P(None, "night", "bl", None),
        P("bl", None),
        P("night"),
        P("night", None),
        P("night", None, None),
        P("night", None),
        P("bl"),
    )
    return jax.shard_map(
        per_device,
        mesh=mesh,
        in_specs=placed,
        out_specs=(P(None, ("night", "bl"), None, None), P(("night", "bl"), None)),
        check_vma=False,
    )
```

profile of v0, /device:TPU:1, one launch (start us, length us, event | category | flops | bytes accessed | tf_op | source)
XLA Modules:
  0.0 130.1 jit_solution(8517169877370450500)
XLA Ops:
  7.2 0.0 all-gather.4.cloned.1.call-start
  7.2 1.5 %copy.25 = f32[2,1,11,768]{3,0,1,2:T(2,128)} copy(f32[2,1,11,768]{3,1,2,0:T(1,128)} %param.13) | data formatting | bytes 135168 | tf_op args[2]
  8.8 0.0 all-gather.4.cloned.1.call-update
  9.4 11.1 %all-gather = s32[4,1,768]{2,1,0:T(1,128)S(1)} all-gather(s32[1,1,768]{2,1,0:T(1,128)} %bitcast.70), channel_id=1, replica_groups=mesh['night'=4,'bl'=32] {'night'}, dimensions={0}, use_global_device_ids=true | all-gather | bytes 15360 | tf_op jit(solution)/shard_map/all_gather | solution.py:44
  20.6 8.2 %all-gather.1 = s32[4,1,32]{2,1,0:T(1,128)S(1)} all-gather(s32[1,1,32]{2,1,0:T(1,128)} %bitcast.73), channel_id=1, replica_groups=mesh['night'=4,'bl'=32] {'night'}, dimensions={0}, use_global_device_ids=true | all-gather | bytes 640 | tf_op jit(solution)/shard_map/all_gather | solution.py:45
  28.8 8.8 %all_gather.18 = f32[4,32,4]{1,2,0:T(4,128)S(1)} all-gather(f32[1,32,4]{1,2,0:T(4,128)} %param.17), channel_id=1, replica_groups=mesh['night'=4,'bl'=32] {'night'}, dimensions={0}, use_global_device_ids=true | all-gather | bytes 2560 | tf_op jit(solution)/shard_map/all_gather | solution.py:48
  37.6 0.8 compare_and_fusion.1
  38.4 0.1 convert_subtract_fusion
  38.5 0.2 select_reduce_fusion
  38.7 0.7 broadcast_multiply_fusion
  39.4 1.1 fusion.19
  40.5 17.8 %all-gather.4.cloned.1.call-done = f32[2,1,352,768]{3,0,1,2:T(2,128)} async-done(((f32[2,1,11,768]{3,0,1,2:T(2,128)}), f32[2,1,352,768]{3,0,1,2:T(2,128)}) %all-gather.4.cloned.1.call-update) | async-done | bytes 2162704 | tf_op jit(solution)/shard_map/all_gather | solution.py:49
  58.4 2.2 %gather_fusion.1 = f32[4,2,768]{2,1,0:T(2,128)S(1)} fusion(f32[2,352,768]{2,0,1:T(2,128)} %bitcast.71, s32[1024]{0:T(1024)S(1)} %pad_clamp_fusion), kind=kCustom, calls=%fused_computation.1.clone | custom fusion | bytes 49168 | tf_op jit(solution)/shard_map/jit(_take)/gather | solution.py:61
  60.6 2.2 %gather_fusion = f32[4,2,768]{2,1,0:T(2,128)S(1)} fusion(f32[2,352,768]{2,0,1:T(2,128)} %bitcast.72, s32[1024]{0:T(1024)S(1)} %pad_clamp_fusion.1), kind=kCustom, calls=%fused_computation.clone | custom fusion | bytes 49168 | tf_op jit(solution)/shard_map/jit(_take)/gather | solution.py:60
  62.8 0.1 select_bitcast_fusion
  62.9 0.1 subtract_multiply_fusion
  63.1 0.8 convolution_bitcast_fusion
  63.9 1.6 %fusion.7 = (f32[1,32,4,768]{3,1,2,0:T(8,128)S(1)}, f32[1,32,4,768]{3,1,2,0:T(8,128)S(1)}) fusion(f32[2,32,4,768]{3,1,2,0:T(8,128)S(1)} %convolution_bitcast_fusion, f32[768]{0:T(1024)S(1)} %multiply_add_fusion.1, f32[32,4]{0,1:T(4,128)S(1)} %broadcast_multiply_fusion), kind=kLoop, calls=%fused_computation.15 | loop fusion | flops 688128 | bytes 1576448 | tf_op jit(solution)/shard_map/sub | solution.py:79
  65.6 0.1 maximum_bitcast_fusion
  65.6 2.5 %broadcast_in_dim.23 = f32[2,128,1,4,768]{4,0,3,2,1:T(2,128)} broadcast(f32[]{:T(128)} %constant.13.clone.1), dimensions={} | broadcast | bytes 3145732 | tf_op jit(solution)/shard_map/broadcast_in_dim | solution.py:84
  68.1 1.5 %copy_dynamic-update-slice_fusion = f32[2,128,1,4,768]{4,0,3,2,1:T(2,128)} fusion(f32[2,128,1,4,768]{4,0,3,2,1:T(2,128)} %broadcast_in_dim.23, s32[]{:T(128)S(6)} %select_n.22, f32[2,32,1,4,768]{4,1,3,0,2:T(8,128)S(1)} %maximum_bitcast_fusion), kind=kLoop, calls=%fused_computation.8 | loop fusion | bytes 1572868 | tf_op jit(solution)/shard_map/dynamic_update_slice | solution.py:85
  69.6 7.1 %all-to-all-start = ((f32[2,128,1,4,768]{4,0,3,2,1:T(2,128)}), f32[2,128,1,4,768]{4,0,3,2,1:T(2,128)S(1)}, u32[]{:S(2)}, u32[]{:S(2)}) async-start(f32[2,128,1,4,768]{4,0,3,2,1:T(2,128)} %copy_dynamic-update-slice_fusion), calls=%async_computation | async-start | bytes 6291456 | tf_op jit(solution)/shard_map/all_to_all | solution.py:87
  76.7 0.6 dynamic-slice
  77.3 0.8 dynamic-update-slice
  78.1 16.6 %all-reduce = s32[4]{0:T(128)S(1)} all-reduce(s32[4]{0:T(128)S(1)} %dynamic-update-slice), channel_id=1, replica_groups=mesh['night'=4,'bl'=32] {'night'}, use_global_device_ids=true, to_apply=%add | all-reduce | flops 4 | bytes 32
  94.7 0.1 fusion.14
  94.8 0.5 fusion.9
  95.3 0.9 fusion.20
  96.1 22.1 %all-to-all-done = f32[2,128,1,4,768]{4,0,3,2,1:T(2,128)S(1)} async-done(((f32[2,128,1,4,768]{4,0,3,2,1:T(2,128)}), f32[2,128,1,4,768]{4,0,3,2,1:T(2,128)S(1)}, u32[]{:S(2)}, u32[]{:S(2)}) %all-to-all-start) | async-done | bytes 3145760 | tf_op jit(solution)/shard_map/all_to_all | solution.py:87
  118.2 2.7 %reduce_sum.21 = f32[2,128,768]{2,0,1:T(2,128)} reduce(f32[2,4,128,768]{3,0,2,1:T(2,128)S(1)} %bitcast.63, f32[]{:T(128)} %constant.13.clone.1), dimensions={1}, to_apply=%region_1.3 | reduce | flops 589824 | bytes 3932164 | tf_op jit(solution)/shard_map/reduce_sum | solution.py:94
  121.0 1.4 %bitcast_divide_fusion = f32[2,1,128,768]{3,0,2,1:T(2,128)S(1)} fusion(f32[2,128,768]{2,0,1:T(2,128)} %reduce_sum.21, f32[768]{0:T(1024)S(1)} %broadcast_maximum_fusion), kind=kLoop, calls=%fused_computation.7 | loop fusion | flops 196608 | bytes 1575936 | tf_op jit(solution)/shard_map/div | solution.py:104
  122.4 0.9 copy.31
  (14 shorter events, 0.1 us)
Async XLA Ops:
  7.2 51.2 %all-gather.4.cloned.1.call-start = ((), (), s32[]{:S(2)}) async-start(), calls=%async_computation.1 | async-start | bytes 2230272 | tf_op jit(solution)/shard_map/all_gather | solution.py:49
  69.6 7.1 %copy-start = (u32[128]{0:T(128)S(1)}, u32[128]{0:T(128)}, u32[]{:S(2)}) copy-start(u32[128]{0:T(128)} %constant.59) | copy-start | bytes 1540
  69.6 48.6 %all-to-all-start = ((f32[2,128,1,4,768]{4,0,3,2,1:T(2,128)}), f32[2,128,1,4,768]{4,0,3,2,1:T(2,128)S(1)}, u32[]{:S(2)}, u32[]{:S(2)}) async-start(f32[2,128,1,4,768]{4,0,3,2,1:T(2,128)} %copy_dynamic-update-slice_fusion), calls=%async_computation | async-start | bytes 6291456 | tf_op jit(solution)/shard_map/all_to_all | solution.py:87
Sparse Core Ops, SparseCore 0:
  10.9 47.4 all-gather.3
where the time goes:
time: 131 us; the launch traced here: 130 us
  blocking collectives  44.7 us (34%)
  waiting for transfers between devices  39.9 us (30%)
  between operations  14.8 us (11%)
  local copies, waits for them, and re-layouts  13.3 us (10%)
  other arithmetic  7.97 us (6%)
  starting transfers between devices  7.14 us (5%)
  matrix products  2.21 us (2%)
    all_to_all x1, waiting for transfers between devices, per_device(): lax.all_to_all(bin_grid.reshape(2, sources, LB_DEV, block_rows, channels)...  22.1 us
    all_gather x1, waiting for transfers between devices, per_device(): gains_all = lax.all_gather(antenna_gain_table, 'bl', axis=2, tiled=True)  17.8 us
    unnamed x1, blocking collectives  16.6 us
    all_gather x1, blocking collectives, per_device(): lax.all_gather(corrupted_sample_markers, 'night', axis=0, tiled=True)  11.1 us
    all_gather x1, blocking collectives, per_device(): weights_all = lax.all_gather(tap_weights, 'night', axis=0, tiled=True)  8.78 us
    all_gather x1, blocking collectives, per_device(): lax.all_gather(tap_offsets, 'night', axis=0, tiled=True)  8.2 us
    all_to_all x1, starting transfers between devices, per_device(): lax.all_to_all(bin_grid.reshape(2, sources, LB_DEV, block_rows, channels)...  7.1 us
    unnamed x9, local copies, waits for them, and re-layouts  3.84 us
  transfers between devices with their start and end apart: 2, of which 2 were waited for; matrix products, arithmetic and copies ran while one was open for 4% of the time, Pallas kernels for 0%

commit v1 on v0

v1 whole, which is shorter than its diff:
```python
import functools
import math

import jax
import jax.numpy as jnp
import numpy as np
from jax import lax
from jax.experimental import pallas as pl
from jax.experimental.pallas import tpu as pltpu
from jax.sharding import PartitionSpec as P

MESH = pl.DeviceIdType.MESH
F32 = jnp.float32
I32 = jnp.int32

NIGHTS = 4
DEVS = 32
BINS = 32
ROWS = 8
CH = 768
SAMPLES = 30
TAPS = 4
OWN_ANT = 11
STAGES = 3
WIDE = 256
HALF = 128
GHALF = 384


def _fit(kind, terms):
    k = np.arange(200)
    u = 0.125 * (1 + np.cos(np.pi * (k + 0.5) / 200))
    r = np.sqrt(u)
    y = np.sin(2 * np.pi * r) / r if kind == "sin" else np.cos(2 * np.pi * r)
    cheb = np.polynomial.chebyshev.Chebyshev.fit(u, y, terms - 1, domain=[0, 0.25])
    return [float(v) for v in cheb.convert(kind=np.polynomial.Polynomial).coef]


SIN_C = _fit("sin", 8)
COS_C = _fit("cos", 8)


def horner(coef, u):
    acc = jnp.full_like(u, coef[-1])
    for c in coef[-2::-1]:
        acc = acc * u + c
    return acc


def swap4(v):
    return pltpu.roll(v, 4, 0)


def flag(cond):
    return jnp.where(cond, jnp.float32(1.0), jnp.float32(0.0))


def comm_kernel(
    vis, gains, imeta_v, fmeta_v, bas_v, fr8, imeta_s, fmeta_s, delay_s,
    landed, wt_ref,
    V, UV, Y, S, gy, gx, bx_v, by_v, bx_s, by_s, m0, m1, c0, c1, G, GZ,
    zi, zf, zis, zfs, s1p, s1n, s2p, s2n, r1p, r1n, r2p, r2n, r3p, r3n,
    local_sem, gsend, gyr, gxr, bsend, bxr, byr, msend, mrecv,
    send0, send1, recv0, recv1, zsend, zrecv, gzs, gzr, asend, arecv,
):
    n = lax.axis_index("night")
    me = lax.axis_index("bl")
    core = lax.rem(me, 2)
    x = lax.rem(me // 2, 4)
    y = me // 8

    def bl_of(yy, xx, cc):
        return (yy * 4 + xx) * 2 + cc

    def rcopy(src, dst, ss, rs, dev):
        return pltpu.make_async_remote_copy(
            src_ref=src, dst_ref=dst, send_sem=ss, recv_sem=rs, device_id=dev, device_id_type=MESH
        )

    load_vis = pltpu.make_async_copy(vis, V, local_sem.at[0])
    load_vis.start()
    own_gy = pltpu.make_async_copy(gains.at[:, :, pl.ds(0, GHALF)], gy.at[y], local_sem.at[1])
    own_gy.start()
    own_gx = pltpu.make_async_copy(gains.at[:, :, pl.ds(GHALF, GHALF)], gx.at[x], local_sem.at[2])
    own_gx.start()

    barrier = pltpu.get_barrier_semaphore()

    def greet_z(k, _):
        pl.semaphore_signal(barrier, inc=1, device_id=(lax.rem(n + k, 4), me), device_id_type=MESH)
        return _

    def greet_bl(k, _):
        pl.semaphore_signal(barrier, inc=1, device_id=(n, lax.rem(me + k, DEVS)), device_id_type=MESH)
        return _

    lax.fori_loop(1, NIGHTS, greet_z, 0)
    lax.fori_loop(1, DEVS, greet_bl, 0)
    pl.semaphore_wait(barrier, NIGHTS - 1 + DEVS - 1)

    zi[n] = imeta_v[...]
    zf[n] = fmeta_v[...]
    bx_v[x * 2 + core] = bas_v[...]
    by_v[y * 2 + core] = bas_v[...]

    def gain_a(k):
        ty = lax.rem(y + k, 4)
        tx = lax.rem(x + k, 4)
        return (
            rcopy(gains.at[:, :, pl.ds(0, GHALF)], gy.at[y], gsend.at[0, k], gyr.at[y], (n, bl_of(ty, x, core))),
            rcopy(gains.at[:, :, pl.ds(GHALF, GHALF)], gx.at[x], gsend.at[1, k], gxr.at[x], (n, bl_of(y, tx, core))),
        )

    for k in (1, 3, 2):
        for c in gain_a(k):
            c.start()

    def slot_dev(k, own):
        s = lax.rem(own + k, 8)
        return s, s // 2, lax.rem(s, 2)

    def bas_x(k):
        s, tx, tc = slot_dev(k, x * 2 + core)
        mine = x * 2 + core
        return rcopy(bas_v, bx_v.at[mine], bsend.at[0, k], bxr.at[mine], (n, bl_of(y, tx, tc)))

    def bas_y(k):
        s, ty, tc = slot_dev(k, y * 2 + core)
        mine = y * 2 + core
        return rcopy(bas_v, by_v.at[mine], bsend.at[1, k], byr.at[mine], (n, bl_of(ty, x, tc)))

    def start_bas(k, _):
        bas_x(k).start()
        bas_y(k).start()
        return _

    lax.fori_loop(1, 8, start_bas, 0)

    def meta(k):
        t = lax.rem(n + k, 4)
        return (
            rcopy(imeta_v, zi.at[n], msend.at[0, k], mrecv.at[0, n], (t, me)),
            rcopy(fmeta_v, zf.at[n], msend.at[1, k], mrecv.at[1, n], (t, me)),
        )

    for k in (1, 3, 2):
        for c in meta(k):
            c.start()

    first = imeta_s[32]

    def shift_of(f, night, e):
        return (lax.shift_right_logical(f, 5) + jnp.where(e < (f & 31), 1, 0) - night) & 3

    lane = lax.broadcasted_iota(I32, (ROWS, WIDE), 1).astype(F32)
    row = lax.broadcasted_iota(I32, (ROWS, WIDE), 0)
    sign = jnp.where(row < 4, jnp.float32(-1.0), jnp.float32(1.0))

    load_vis.wait()

    def prepare(st):
        at = st * WIDE

        def per_sample(t, _):
            bits = (imeta_v[:, pl.ds(HALF + at, WIDE)] >> t) & 1
            keep = 1.0 - bits.astype(F32)
            for i in range(ROWS):
                UV[t, pl.ds(i, 1), pl.ds(at, WIDE)] = V[i // 4, i % 4, pl.ds(t, 1), pl.ds(at, WIDE)] * keep
            return _

        lax.fori_loop(0, SAMPLES, per_sample, 0)
        freq = 1.0 + (lane + float(at)) * (1.0 / CH)
        rate = fr8[...] * freq

        def per_bin(e, _):
            l = (e - first) & 31
            off = imeta_s[l]
            acc = fmeta_s[l * 4] * UV[off, :, pl.ds(at, WIDE)]
            for k in range(1, TAPS):
                acc = acc + fmeta_s[l * 4 + k] * UV[off + k, :, pl.ds(at, WIDE)]
            turns = rate * delay_s[l]
            r = turns - jnp.floor(turns + 0.5)
            u = r * r
            sine = horner(SIN_C, u) * (r * sign)
            cosine = horner(COS_C, u)
            Y[st, e] = cosine * acc + sine * swap4(acc)
            return _

        lax.fori_loop(0, BINS, per_bin, 0)

    up = lax.rem(n + 1, 4)
    down = lax.rem(n + 3, 4)
    far = lax.rem(n + 2, 4)

    def zcopy(st, which):
        src = (s1p, s1n, s2p, s2n)[which]
        dst = (r1p, r1n, r2p, r2n)[which]
        to = up if which % 2 == 0 else down
        return rcopy(src.at[st], dst.at[st], zsend.at[st, which], zrecv.at[st, which], (to, me))

    def forward(which):
        src, dst = ((r1p, r3p), (r1n, r3n))[which]
        to = (up, down)[which]
        return rcopy(src.at[0], dst, zsend.at[STAGES, which], zrecv.at[STAGES, which], (to, me))

    lo = pl.ds(0, HALF)
    hi = pl.ds(HALF, HALF)

    def build_first(st):
        def per_bin(e, _):
            s = shift_of(first, n, e)
            a, b = Y[st, e, :, lo], Y[st, e, :, hi]
            two = flag(s == 2)
            s1p[st, e] = two * a + flag(s == 1) * b
            s1n[st, e] = two * b + flag(s == 3) * a
            return _

        lax.fori_loop(0, BINS, per_bin, 0)

    prepare(0)
    build_first(0)
    zcopy(0, 0).start()
    zcopy(0, 1).start()

    def early_second(e, _):
        s = shift_of(first, n, e)
        s2p[0, e] = flag(s == 1) * Y[0, e, :, lo]
        s2n[0, e] = flag(s == 3) * Y[0, e, :, hi]
        return _

    lax.fori_loop(0, BINS, early_second, 0)
    zcopy(0, 2).start()
    zcopy(0, 3).start()

    def wait_bas(k, _):
        sx = lax.rem(x * 2 + core + k, 8)
        sy = lax.rem(y * 2 + core + k, 8)
        rcopy(bas_v, bx_v.at[sx], bsend.at[0, k], bxr.at[sx], (n, me)).wait_recv()
        rcopy(bas_v, by_v.at[sy], bsend.at[1, k], byr.at[sy], (n, me)).wait_recv()
        return _

    lax.fori_loop(1, 8, wait_bas, 0)
    to_s0 = pltpu.make_async_copy(bx_v, bx_s, local_sem.at[3])
    to_s1 = pltpu.make_async_copy(by_v, by_s, local_sem.at[4])
    to_s0.start()
    to_s1.start()
    own_gy.wait()
    own_gx.wait()
    for k in (1, 2, 3):
        sy, sx = lax.rem(y + k, 4), lax.rem(x + k, 4)
        rcopy(gy.at[sy], gy.at[sy], gsend.at[0, k], gyr.at[sy], (n, me)).wait_recv()
        rcopy(gx.at[sx], gx.at[sx], gsend.at[1, k], gxr.at[sx], (n, me)).wait_recv()
    to_s0.wait()
    to_s1.wait()

    def pick(slot, asked, table, out, mine_a, along):
        for r in range(ROWS):
            a = asked[slot, 0, r]
            owner = a // OWN_ANT
            at = a - owner * OWN_ANT
            oc = owner & 1
            ox = (owner >> 1) & 3
            oy = owner >> 3
            fixed, moving = (ox, oy) if along == 0 else (oy, ox)
            w = flag((fixed == mine_a) & (oc == core))
            for p in range(2):
                out[slot, p, pl.ds(r, 1), :] = w * table[moving, p, pl.ds(at, 1), :]

    def gain_b0(k):
        s, tx, tc = slot_dev(k, x * 2 + core)
        mine = x * 2 + core
        return rcopy(m0.at[s], c0.at[mine], send0.at[k], recv0.at[mine], (n, bl_of(y, tx, tc)))

    def gain_b1(k):
        s, ty, tc = slot_dev(k, y * 2 + core)
        mine = y * 2 + core
        return rcopy(m1.at[s], c1.at[mine], send1.at[k], recv1.at[mine], (n, bl_of(ty, x, tc)))

    def send_rows(k, _):
        pick(lax.rem(x * 2 + core + k, 8), bx_s, gy, m0, x, 0)
        gain_b0(k).start()
        pick(lax.rem(y * 2 + core + k, 8), by_s, gx, m1, y, 1)
        gain_b1(k).start()
        return _

    lax.fori_loop(1, 8, send_rows, 0)
    pick(x * 2 + core, bx_s, gy, m0, x, 0)
    pick(y * 2 + core, by_s, gx, m1, y, 1)
    c0[x * 2 + core] = m0[x * 2 + core]
    c1[y * 2 + core] = m1[y * 2 + core]

    for k in (1, 2, 3):
        o = lax.rem(n + k, 4)
        rcopy(imeta_v, zi.at[o], msend.at[0, k], mrecv.at[0, o], (n, me)).wait_recv()
        rcopy(fmeta_v, zf.at[o], msend.at[1, k], mrecv.at[1, o], (n, me)).wait_recv()
    to_s2 = pltpu.make_async_copy(zi.at[:, :, pl.ds(0, HALF)], zis, local_sem.at[5])
    to_s3 = pltpu.make_async_copy(zf, zfs, local_sem.at[6])
    to_s2.start()
    to_s3.start()

    for w in (0, 1):
        zcopy(0, w).wait_recv()
        forward(w).start()

    prepare(1)
    prepare(2)

    to_s2.wait()
    to_s3.wait()
    first_down, first_up, first_far = zis[down, 0, 32], zis[up, 0, 32], zis[far, 0, 32]

    total = jnp.zeros((1, CH), F32)
    bin_here = n * BINS + me
    for k in range(NIGHTS):
        l = bin_here - zis[k, 0, 32]
        valid = flag((l >= 0) & (l < BINS))
        lc = jnp.clip(l, 0, BINS - 1)
        off = zis[k, 0, lc]
        for t in range(TAPS):
            bits = (zi[k, :, pl.ds(HALF, CH)] >> (off + t)) & 1
            total = total + (valid * zfs[k, 0, lc * 4 + t]) * (1.0 - bits.astype(F32))
    wt_ref[...] = total

    def wait_rows(k, _):
        sx = lax.rem(x * 2 + core + k, 8)
        sy = lax.rem(y * 2 + core + k, 8)
        rcopy(m0.at[sx], c0.at[sx], send0.at[k], recv0.at[sx], (n, me)).wait_recv()
        rcopy(m1.at[sy], c1.at[sy], send1.at[k], recv1.at[sy], (n, me)).wait_recv()
        return _

    lax.fori_loop(1, 8, wait_rows, 0)
    for h, c in ((0, c0), (1, c1)):
        parts = []
        for p in range(2):
            acc = c[0, p]
            for s in range(1, 8):
                acc = acc + c[s, p]
            parts.append(acc)
        A, B = parts
        G[0, :, pl.ds(h * GHALF, GHALF)] = A * swap4(A) + B * swap4(B)
        G[1, :, pl.ds(h * GHALF, GHALF)] = A * swap4(B) - B * swap4(A)
    GZ[n] = G[:, :, pl.ds(0, WIDE)]

    def gz(k):
        return rcopy(GZ.at[n], GZ.at[n], gzs.at[k], gzr.at[n], (lax.rem(n + k, 4), me))

    for k in (1, 3, 2):
        gz(k).start()

    for st in (1, 2):
        gr, gs = G[0, :, pl.ds(st * WIDE, WIDE)], G[1, :, pl.ds(st * WIDE, WIDE)]

        def apply(e, _, st=st, gr=gr, gs=gs):
            v = Y[st, e]
            v = gr * v + gs * swap4(v)
            Y[st, e] = v
            s = shift_of(first, n, e)
            a, b = v[:, :HALF], v[:, HALF:]
            two = flag(s == 2)
            s1p[st, e] = two * a + flag(s == 1) * b
            s1n[st, e] = two * b + flag(s == 3) * a
            return _

        lax.fori_loop(0, BINS, apply, 0)
        zcopy(st, 0).start()
        zcopy(st, 1).start()

    for st in (1, 2):
        zcopy(st, 0).wait_recv()
        zcopy(st, 1).wait_recv()

        def second(e, _, st=st):
            s = shift_of(first, n, e)
            s2p[st, e] = flag(s == 1) * Y[st, e, :, lo] + flag(shift_of(first_down, down, e) == 2) * r1p[st, e]
            s2n[st, e] = flag(s == 3) * Y[st, e, :, hi] + flag(shift_of(first_up, up, e) == 2) * r1n[st, e]
            return _

        lax.fori_loop(0, BINS, second, 0)
        zcopy(st, 2).start()
        zcopy(st, 3).start()

    def bin_copy(st, k):
        t = lax.rem(me + k, DEVS)
        return rcopy(S.at[st, t], landed.at[st, me], asend.at[st], arecv.at[st], (n, t))

    def send_bins(st):
        def go(k, _):
            bin_copy(st, k).start()
            return _

        lax.fori_loop(1, DEVS, go, 0)
        landed[st, me] = S[st, me]

    for k in (1, 2, 3):
        o = lax.rem(n + k, 4)
        rcopy(GZ.at[o], GZ.at[o], gzs.at[k], gzr.at[o], (n, me)).wait_recv()
    zcopy(0, 2).wait_recv()
    zcopy(0, 3).wait_recv()
    forward(0).wait_recv()
    forward(1).wait_recv()

    def combine0(e, _):
        here = flag(shift_of(first, n, e) == 0)
        from_down = flag(shift_of(first_down, down, e) == 1)
        from_up = flag(shift_of(first_up, up, e) == 3)
        from_far = flag(shift_of(first_far, far, e) == 2)

        def part(half, terms):
            acc = None
            for night, v in terms:
                w = GZ[night, 0, :, half] * v + GZ[night, 1, :, half] * swap4(v)
                acc = w if acc is None else acc + w
            S[0, e, :, half] = acc

        part(lo, ((n, here * Y[0, e, :, lo]), (up, from_up * r1n[0, e]), (down, r2p[0, e]), (far, from_far * r3p[e])))
        part(hi, ((n, here * Y[0, e, :, hi]), (down, from_down * r1p[0, e]), (up, r2n[0, e]), (far, from_far * r3n[e])))
        return _

    lax.fori_loop(0, BINS, combine0, 0)
    send_bins(0)

    for st in (1, 2):
        zcopy(st, 2).wait_recv()
        zcopy(st, 3).wait_recv()

        def combine(e, _, st=st):
            here = flag(shift_of(first, n, e) == 0)
            from_down = flag(shift_of(first_down, down, e) == 1)
            from_up = flag(shift_of(first_up, up, e) == 3)
            S[st, e, :, lo] = here * Y[st, e, :, lo] + from_up * r1n[st, e] + r2p[st, e]
            S[st, e, :, hi] = here * Y[st, e, :, hi] + from_down * r1p[st, e] + r2n[st, e]
            return _

        lax.fori_loop(0, BINS, combine, 0)
        send_bins(st)

    for k in (1, 2, 3):
        for c in gain_a(k):
            c.wait_send()
        for c in meta(k):
            c.wait_send()
        gz(k).wait_send()

    def done(k, _):
        bas_x(k).wait_send()
        bas_y(k).wait_send()
        gain_b0(k).wait_send()
        gain_b1(k).wait_send()
        return _

    lax.fori_loop(1, 8, done, 0)
    for st in range(STAGES):
        for w in range(4):
            zcopy(st, w).wait_send()
    for w in (0, 1):
        forward(w).wait_send()
    for st in range(STAGES):
        whole = rcopy(
            S.at[st, pl.ds(0, DEVS - 1)], landed.at[st, pl.ds(0, DEVS - 1)], asend.at[st], arecv.at[st], (n, me)
        )
        whole.wait_send()
        whole.wait_recv()


def final_kernel(landed, wt, out, wt_out):
    row = lax.broadcasted_iota(I32, (ROWS, WIDE), 0)
    low = row < 4
    wt_out[...] = wt[...]
    for st in range(STAGES):
        cols = pl.ds(st * WIDE, WIDE)
        inv = jnp.broadcast_to(1.0 / jnp.maximum(wt[:, cols], 0.5), (ROWS, WIDE))

        def pair(k, _, st=st, cols=cols, inv=inv):
            a = landed[st, 2 * k] * inv
            b = landed[st, 2 * k + 1] * inv
            at = pl.multiple_of(k * 8, 8)
            out[0, pl.ds(at, 8), cols] = jnp.where(low, a, swap4(b))
            out[1, pl.ds(at, 8), cols] = jnp.where(low, swap4(a), b)
            return _

        lax.fori_loop(0, DEVS // 2, pair, 0)


def per_device(
    visibilities, corrupted_sample_markers, antenna_gain_table, baseline_antennas, first_bin, tap_offsets, tap_weights,
    lst_delay, fringe_rate,
):
    vis = visibilities.reshape(2, 4, SAMPLES, CH)
    gains = antenna_gain_table.reshape(2, OWN_ANT, CH)
    small = jnp.concatenate([tap_offsets.reshape(32), first_bin, jnp.zeros((95,), I32)])
    imeta = jnp.concatenate([small, corrupted_sample_markers.reshape(CH)]).reshape(1, HALF + CH)
    fmeta = tap_weights.reshape(1, HALF)
    bas = jnp.concatenate([baseline_antennas.T.reshape(8), jnp.zeros((120,), I32)]).reshape(1, HALF)
    fr8 = jnp.broadcast_to(jnp.tile(fringe_rate * (1.0 / (2.0 * math.pi)), 2)[:, None], (ROWS, WIDE))

    vm = pl.BlockSpec(memory_space=pltpu.VMEM)
    sm = pl.BlockSpec(memory_space=pltpu.SMEM)
    hbm = pl.BlockSpec(memory_space=pl.ANY)
    D = pltpu.SemaphoreType.DMA
    msg = (STAGES, BINS, ROWS, HALF)
    landed, wt = pl.pallas_call(
        comm_kernel,
        out_shape=(
            jax.ShapeDtypeStruct((STAGES, DEVS, ROWS, WIDE), F32),
            jax.ShapeDtypeStruct((1, CH), F32),
        ),
        in_specs=[hbm, hbm, vm, vm, vm, vm, sm, sm, sm],
        out_specs=(vm, vm),
        scratch_shapes=[
            pltpu.VMEM((2, 4, SAMPLES, CH), F32),
            pltpu.VMEM((SAMPLES, ROWS, CH), F32),
            pltpu.VMEM((STAGES, BINS, ROWS, WIDE), F32),
            pltpu.VMEM((STAGES, BINS, ROWS, WIDE), F32),
            pltpu.VMEM((4, 2, OWN_ANT, GHALF), F32),
            pltpu.VMEM((4, 2, OWN_ANT, GHALF), F32),
            pltpu.VMEM((8, 1, HALF), I32),
            pltpu.VMEM((8, 1, HALF), I32),
            pltpu.SMEM((8, 1, HALF), I32),
            pltpu.SMEM((8, 1, HALF), I32),
            pltpu.VMEM((8, 2, ROWS, GHALF), F32),
            pltpu.VMEM((8, 2, ROWS, GHALF), F32),
            pltpu.VMEM((8, 2, ROWS, GHALF), F32),
            pltpu.VMEM((8, 2, ROWS, GHALF), F32),
            pltpu.VMEM((2, ROWS, CH), F32),
            pltpu.VMEM((NIGHTS, 2, ROWS, WIDE), F32),
            pltpu.VMEM((NIGHTS, 1, HALF + CH), I32),
            pltpu.VMEM((NIGHTS, 1, HALF), F32),
            pltpu.SMEM((NIGHTS, 1, HALF), I32),
            pltpu.SMEM((NIGHTS, 1, HALF), F32),
        ]
        + [pltpu.VMEM(msg, F32)] * 8
        + [pltpu.VMEM(msg[1:], F32)] * 2
        + [
            D((7,)), D((2, 4)), D((4,)), D((4,)), D((2, 8)), D((8,)), D((8,)), D((2, 4)), D((2, 4)),
            D((8,)), D((8,)), D((8,)), D((8,)), D((STAGES + 1, 4)), D((STAGES + 1, 4)), D((4,)), D((4,)),
            D((STAGES,)), D((STAGES,)),
        ],
        compiler_params=pltpu.CompilerParams(
            collective_id=0, has_side_effects=True, vmem_limit_bytes=40 * 1024 * 1024
        ),
        name="exchange",
    )(vis, gains, imeta, fmeta, bas, fr8, small, fmeta.reshape(HALF), lst_delay.reshape(BINS))

    binned, weight_total = pl.pallas_call(
        final_kernel,
        out_shape=(jax.ShapeDtypeStruct((2, 4 * DEVS, CH), F32), jax.ShapeDtypeStruct((1, CH), F32)),
        in_specs=[vm, vm],
        out_specs=(vm, vm),
        compiler_params=pltpu.CompilerParams(vmem_limit_bytes=16 * 1024 * 1024),
        name="assemble",
    )(landed, wt)
    return binned.reshape(2, 1, 4 * DEVS, CH), weight_total


def solution(mesh):
    placed = (
        P(None, "night", "bl", None, None),
        P("night", None),
        P(None, "night", "bl", None),
        P("bl", None),
        P("night"),
        P("night", None),
        P("night", None, None),
        P("night", None),
        P("bl"),
    )
    return jax.shard_map(
        per_device,
        mesh=mesh,
        in_specs=placed,
        out_specs=(P(None, ("night", "bl"), None, None), P(("night", "bl"), None)),
        check_vma=False,
    )
```

time: 131 us -> 53.2 us (0.41)
  Pallas kernels: 0 us -> 44.8 us
  blocking collectives: 44.7 us -> 0 us
  waiting for transfers between devices: 39.9 us -> 0 us
  between operations: 14.8 us -> 1.38 us
  local copies, waits for them, and re-layouts: 13.3 us -> 3.88 us
  starting transfers between devices: 7.14 us -> 0 us
  other arithmetic: 7.97 us -> 2.82 us
  matrix products: 2.21 us -> 0 us
    pallas_call x0 -> x2, Pallas kernels: none -> 44.8 us  [the longest x1 43.6 us: per_device(): pl.pallas_call(comm_kernel, out_shape=(jax.ShapeDtypeStruct((STAGES, DEVS...]
    all_gather x3 -> x0, blocking collectives: 28.1 us -> none  [the longest x1 11.1 us: per_device(): lax.all_gather(corrupted_sample_markers, 'night', axis=0, tiled=True)]
    all_to_all x1 -> x0, waiting for transfers between devices: 22.1 us -> none  [per_device(): lax.all_to_all(bin_grid.reshape(2, sources, LB_DEV, block_rows, channels)...]
    all_gather x1 -> x0, waiting for transfers between devices: 17.8 us -> none  [per_device(): gains_all = lax.all_gather(antenna_gain_table, 'bl', axis=2, tiled=True)]
    unnamed x1 -> x0, blocking collectives: 16.6 us -> none
    all_to_all x1 -> x0, starting transfers between devices: 7.1 us -> none  [per_device(): lax.all_to_all(bin_grid.reshape(2, sources, LB_DEV, block_rows, channels)...]
    gather x2 -> x0, local copies, waits for them, and re-layouts: 4.38 us -> none  [the longest x1 2.19 us: per_device(): first_gain = jnp.take(gains_all[:, 0], baseline_antennas[:, 0], axis=1)]
    reduce_sum x2 -> x0, other arithmetic: 2.93 us -> none  [the longest x1 2.75 us: per_device(): jnp.sum(arrived.reshape(2, LB_DEV, night_count, block_count * block_rows,...]
  transfers between devices with their start and end apart: 2 -> 0, of which waited for: 2 -> 0; matrix products, arithmetic and copies ran while one was open for 4% -> 0% of each run, Pallas kernels for 0% -> 0%
where the time goes in v1:
time: 53.2 us; the launch traced here: 52.9 us
  Pallas kernels  44.8 us (84%)
  local copies, waits for them, and re-layouts  3.88 us (7%)
  other arithmetic  2.82 us (5%)
  between operations  1.38 us (3%)
    pallas_call x1, Pallas kernels, per_device(): pl.pallas_call(comm_kernel, out_shape=(jax.ShapeDtypeStruct((STAGES, DEVS...  43.6 us
    unnamed x7, local copies, waits for them, and re-layouts  2.73 us
    pallas_call x1, Pallas kernels, per_device(): pl.pallas_call(final_kernel, out_shape=(jax.ShapeDtypeStruct((2, 4 * DEVS...  1.22 us

profile of v1, /device:TPU:1, one launch (start us, length us, event | category | flops | bytes accessed | tf_op | source)
XLA Modules:
  0.0 52.9 jit_solution(3955967240881075439)
XLA Ops:
  0.6 0.0 copy-start.1
  1.3 0.7 %pad_add_fusion.1.imeta_s = s32[128]{0:T(128)S(1)} fusion(s32[95]{0:T(128)S(1)} %broadcast_in_dim.11, s32[1]{0:T(128)S(6)} %copy.25, s32[32]{0:T(128)} %bitcast.17), kind=kLoop, calls=%fused_computation.3 | loop fusion | flops 256 | bytes 1024 | tf_op jit(solution)/shard_map/concatenate | solution.py:490
  2.1 0.8 %reshape.42 = s32[8]{0:T(128)S(1)} reshape(s32[2,4]{1,0:T(2,128)} %bitcast.20) | data formatting | bytes 64 | tf_op jit(solution)/shard_map/reshape | solution.py:493
  2.8 0.7 %broadcast_multiply_fusion = f32[4]{0:T(128)S(1)} fusion(f32[4]{0:T(128)} %param.17), kind=kLoop, calls=%fused_computation.5 | loop fusion | flops 4 | bytes 32 | tf_op jit(solution)/shard_map/mul | solution.py:494
  3.5 0.1 broadcast_in_dim.12
  3.6 0.7 %reduce = s32[768]{0:T(1024)S(1)} reduce(s32[1,768]{1,0:T(1,128)} %param.10, s32[]{:T(128)} %constant.2.clone.1), dimensions={0}, to_apply=%param.10.reduce_sub_computation | reduce | bytes 6148 | tf_op args[1]
  4.3 0.7 %pad_add_fusion = s32[896]{0:T(1024)S(1)} fusion(s32[768]{0:T(1024)S(1)} %reduce, s32[95]{0:T(128)S(1)} %broadcast_in_dim.11, s32[1]{0:T(128)S(6)} %copy.25, s32[32]{0:T(128)} %bitcast.18), kind=kLoop, calls=%fused_computation.2 | loop fusion | flops 2688 | bytes 7168 | tf_op jit(solution)/shard_map/concatenate | solution.py:491
  5.0 0.1 broadcast_in_dim.13.fr8
  5.1 0.8 %copy.17 = f32[1,32,4]{2,1,0:T(8,128)S(1)} copy(f32[1,32,4]{1,2,0:T(4,128)} %param.15) | data formatting | bytes 1024 | tf_op args[6]
  5.9 0.1 reshape_reshape.3.fmeta_s
  6.0 0.1 reshape.41.fmeta_v
  6.1 0.0 copy-done.1
  6.1 1.3 %copy.23 = f32[2,1,4,30,768]{4,3,2,0,1:T(8,128)S(1)} copy(f32[2,1,4,30,768]{4,2,3,1,0:T(4,128)} %param.9) | data formatting | bytes 1474560 | tf_op args[0]
  7.4 0.0 copy-start
  7.4 0.6 %copy-done = f32[1,32]{1,0:T(1,128)S(1)} copy-done((f32[1,32]{1,0:T(1,128)S(1)}, f32[1,32]{1,0:T(1,128)}, u32[]{:S(2)}) %copy-start) | copy-done | bytes 152
  8.1 43.6 %exchange.1 = (f32[3,32,8,256]{3,2,1,0:T(8,128)S(1)}, f32[1,768]{1,0:T(1,128)S(1)}) custom-call(f32[2,4,30,768]{3,2,1,0:T(8,128)S(1)} %bitcast.14, f32[2,11,768]{2,1,0:T(8,128)S(1)} %copy.19.gains, s32[1,896]{1,0:T(1,128)S(1)} %reshape.40.imeta_v, f32[1,128]{1,0:T(1,128)S(1)} %reshape.41.fmeta_v, s32[1,128]{1,0:T(1,128)S(1)} %pad_bitcast_fusion.bas_v, ...), custom_call_target="tpu_custom_call" | custom-call | tf_op jit(solution)/shard_map/exchange/pallas_call | solution.py:501
  51.7 1.2 %assemble.1 = (f32[2,128,768]{2,1,0:T(8,128)}, f32[1,768]{1,0:T(1,128)}) custom-call(f32[3,32,8,256]{3,2,1,0:T(8,128)S(1)} %get-tuple-element.6.landed, f32[1,768]{1,0:T(1,128)S(1)} %get-tuple-element.7.wt), custom_call_target="tpu_custom_call" | custom-call | tf_op jit(solution)/shard_map/assemble/pallas_call | solution.py:544
  (6 shorter events, 0.1 us)
Async XLA Ops:
  0.6 5.4 %copy-start.1 = (f32[2,1,11,768]{3,1,2,0:T(1,128)S(1)}, f32[2,1,11,768]{3,1,2,0:T(1,128)}, u32[]{:S(2)}) copy-start(f32[2,1,11,768]{3,1,2,0:T(1,128)} %param.11) | copy-start | bytes 202756
  7.4 0.7 %copy-start = (f32[1,32]{1,0:T(1,128)S(1)}, f32[1,32]{1,0:T(1,128)}, u32[]{:S(2)}) copy-start(f32[1,32]{1,0:T(1,128)} %param.16) | copy-start | bytes 388

commit v2 on v1

--- a/solution.py
+++ b/solution.py
@@ -56,10 +56,10 @@
 
 
 def comm_kernel(
-    vis, gains, imeta_v, fmeta_v, bas_v, fr8, imeta_s, fmeta_s, delay_s,
+    vis, gains, flags_h, offs_h, first_h, weights_h, delay_h, bas_h, rate_h,
     landed, wt_ref,
-    V, UV, Y, S, gy, gx, bx_v, by_v, bx_s, by_s, m0, m1, c0, c1, G, GZ,
-    zi, zf, zis, zfs, s1p, s1n, s2p, s2n, r1p, r1n, r2p, r2n, r3p, r3n,
+    offs_s, first_s, weights_s, delay_s, rate_s, V, UV, Y, S, gy, gx, bx_v, by_v, bx_s, by_s, m0, m1, c0, c1, G, GZ,
+    zflags, zfirst, zoffs, zw, zfirst_s, zoffs_s, zw_s, s1p, s1n, s2p, s2n, r1p, r1n, r2p, r2n, r3p, r3n,
     local_sem, gsend, gyr, gxr, bsend, bxr, byr, msend, mrecv,
     send0, send1, recv0, recv1, zsend, zrecv, gzs, gzr, asend, arecv,
 ):
@@ -78,11 +78,20 @@
         )
 
     load_vis = pltpu.make_async_copy(vis, V, local_sem.at[0])
-    load_vis.start()
-    own_gy = pltpu.make_async_copy(gains.at[:, :, pl.ds(0, GHALF)], gy.at[y], local_sem.at[1])
-    own_gy.start()
-    own_gx = pltpu.make_async_copy(gains.at[:, :, pl.ds(GHALF, GHALF)], gx.at[x], local_sem.at[2])
-    own_gx.start()
+    own_gy = pltpu.make_async_copy(gains.at[:, :, :, pl.ds(0, GHALF)], gy.at[y], local_sem.at[1])
+    own_gx = pltpu.make_async_copy(gains.at[:, :, :, pl.ds(GHALF, GHALF)], gx.at[x], local_sem.at[2])
+    small = [
+        pltpu.make_async_copy(a, b, local_sem.at[7 + i])
+        for i, (a, b) in enumerate(
+            (
+                (first_h, first_s), (offs_h, offs_s), (weights_h, weights_s), (delay_h, delay_s), (rate_h, rate_s),
+                (flags_h, zflags.at[n]), (offs_h, zoffs.at[n]), (weights_h, zw.at[n]),
+                (bas_h, bx_v.at[x * 2 + core]), (bas_h, by_v.at[y * 2 + core]),
+            )
+        )
+    ]
+    for c in (*small, load_vis, own_gy, own_gx):
+        c.start()
 
     barrier = pltpu.get_barrier_semaphore()
 
@@ -97,18 +106,13 @@
     lax.fori_loop(1, NIGHTS, greet_z, 0)
     lax.fori_loop(1, DEVS, greet_bl, 0)
     pl.semaphore_wait(barrier, NIGHTS - 1 + DEVS - 1)
-
-    zi[n] = imeta_v[...]
-    zf[n] = fmeta_v[...]
-    bx_v[x * 2 + core] = bas_v[...]
-    by_v[y * 2 + core] = bas_v[...]
 
     def gain_a(k):
         ty = lax.rem(y + k, 4)
         tx = lax.rem(x + k, 4)
         return (
-            rcopy(gains.at[:, :, pl.ds(0, GHALF)], gy.at[y], gsend.at[0, k], gyr.at[y], (n, bl_of(ty, x, core))),
-            rcopy(gains.at[:, :, pl.ds(GHALF, GHALF)], gx.at[x], gsend.at[1, k], gxr.at[x], (n, bl_of(y, tx, core))),
+            rcopy(gains.at[:, :, :, pl.ds(0, GHALF)], gy.at[y], gsend.at[0, k], gyr.at[y], (n, bl_of(ty, x, core))),
+            rcopy(gains.at[:, :, :, pl.ds(GHALF, GHALF)], gx.at[x], gsend.at[1, k], gxr.at[x], (n, bl_of(y, tx, core))),
         )
 
     for k in (1, 3, 2):
@@ -122,12 +126,12 @@
     def bas_x(k):
         s, tx, tc = slot_dev(k, x * 2 + core)
         mine = x * 2 + core
-        return rcopy(bas_v, bx_v.at[mine], bsend.at[0, k], bxr.at[mine], (n, bl_of(y, tx, tc)))
+        return rcopy(bas_h, bx_v.at[mine], bsend.at[0, k], bxr.at[mine], (n, bl_of(y, tx, tc)))
 
     def bas_y(k):
         s, ty, tc = slot_dev(k, y * 2 + core)
         mine = y * 2 + core
-        return rcopy(bas_v, by_v.at[mine], bsend.at[1, k], byr.at[mine], (n, bl_of(ty, x, tc)))
+        return rcopy(bas_h, by_v.at[mine], bsend.at[1, k], byr.at[mine], (n, bl_of(ty, x, tc)))
 
     def start_bas(k, _):
         bas_x(k).start()
@@ -136,19 +140,27 @@
 
     lax.fori_loop(1, 8, start_bas, 0)
 
+    for c in small:
+        c.wait()
+    first = first_s[0]
+    zfirst[n] = jnp.full((1, HALF), first, I32)
+
     def meta(k):
         t = lax.rem(n + k, 4)
-        return (
-            rcopy(imeta_v, zi.at[n], msend.at[0, k], mrecv.at[0, n], (t, me)),
-            rcopy(fmeta_v, zf.at[n], msend.at[1, k], mrecv.at[1, n], (t, me)),
-        )
+        return [
+            rcopy(a, b, msend.at[i, k], mrecv.at[i, n], (t, me))
+            for i, (a, b) in enumerate(
+                (
+                    (flags_h, zflags.at[n]), (offs_h, zoffs.at[n]), (weights_h, zw.at[n]),
+                    (zfirst.at[n], zfirst.at[n]),
+                )
+            )
+        ]
 
     for k in (1, 3, 2):
         for c in meta(k):
             c.start()
 
-    first = imeta_s[32]
-
     def shift_of(f, night, e):
         return (lax.shift_right_logical(f, 5) + jnp.where(e < (f & 31), 1, 0) - night) & 3
 
@@ -156,29 +168,33 @@
     row = lax.broadcasted_iota(I32, (ROWS, WIDE), 0)
     sign = jnp.where(row < 4, jnp.float32(-1.0), jnp.float32(1.0))
 
+    which = row & 3
+    rates = jnp.where(
+        which < 2, jnp.where(which == 0, rate_s[0], rate_s[1]), jnp.where(which == 2, rate_s[2], rate_s[3])
+    ) * (1.0 / (2.0 * math.pi))
+
     load_vis.wait()
 
     def prepare(st):
         at = st * WIDE
 
         def per_sample(t, _):
-            bits = (imeta_v[:, pl.ds(HALF + at, WIDE)] >> t) & 1
-            keep = 1.0 - bits.astype(F32)
-            for i in range(ROWS):
-                UV[t, pl.ds(i, 1), pl.ds(at, WIDE)] = V[i // 4, i % 4, pl.ds(t, 1), pl.ds(at, WIDE)] * keep
+            bits = (zflags[n, :, pl.ds(at, WIDE)] >> t) & 1
+            both = jnp.concatenate([V[0, t, :, pl.ds(at, WIDE)], V[1, t, :, pl.ds(at, WIDE)]], axis=0)
+            UV[t, :, pl.ds(at, WIDE)] = both * (1.0 - bits.astype(F32))
             return _
 
         lax.fori_loop(0, SAMPLES, per_sample, 0)
         freq = 1.0 + (lane + float(at)) * (1.0 / CH)
-        rate = fr8[...] * freq
+        rate = rates * freq
 
         def per_bin(e, _):
             l = (e - first) & 31
-            off = imeta_s[l]
-            acc = fmeta_s[l * 4] * UV[off, :, pl.ds(at, WIDE)]
+            off = offs_s[0, l]
+            acc = weights_s[0, l] * UV[off, :, pl.ds(at, WIDE)]
             for k in range(1, TAPS):
-                acc = acc + fmeta_s[l * 4 + k] * UV[off + k, :, pl.ds(at, WIDE)]
-            turns = rate * delay_s[l]
+                acc = acc + weights_s[k, l] * UV[off + k, :, pl.ds(at, WIDE)]
+            turns = rate * delay_s[0, l]
             r = turns - jnp.floor(turns + 0.5)
             u = r * r
             sine = horner(SIN_C, u) * (r * sign)
@@ -235,8 +251,8 @@
     def wait_bas(k, _):
         sx = lax.rem(x * 2 + core + k, 8)
         sy = lax.rem(y * 2 + core + k, 8)
-        rcopy(bas_v, bx_v.at[sx], bsend.at[0, k], bxr.at[sx], (n, me)).wait_recv()
-        rcopy(bas_v, by_v.at[sy], bsend.at[1, k], byr.at[sy], (n, me)).wait_recv()
+        rcopy(bas_h, bx_v.at[sx], bsend.at[0, k], bxr.at[sx], (n, me)).wait_recv()
+        rcopy(bas_h, by_v.at[sy], bsend.at[1, k], byr.at[sy], (n, me)).wait_recv()
         return _
 
     lax.fori_loop(1, 8, wait_bas, 0)
@@ -255,7 +271,7 @@
 
     def pick(slot, asked, table, out, mine_a, along):
         for r in range(ROWS):
-            a = asked[slot, 0, r]
+            a = asked[slot, r // 4, r % 4]
             owner = a // OWN_ANT
             at = a - owner * OWN_ANT
             oc = owner & 1
@@ -264,7 +280,7 @@
             fixed, moving = (ox, oy) if along == 0 else (oy, ox)
             w = flag((fixed == mine_a) & (oc == core))
             for p in range(2):
-                out[slot, p, pl.ds(r, 1), :] = w * table[moving, p, pl.ds(at, 1), :]
+                out[slot, p, pl.ds(r, 1), :] = w * table[moving, p, at]
 
     def gain_b0(k):
         s, tx, tc = slot_dev(k, x * 2 + core)
@@ -291,12 +307,16 @@
 
     for k in (1, 2, 3):
         o = lax.rem(n + k, 4)
-        rcopy(imeta_v, zi.at[o], msend.at[0, k], mrecv.at[0, o], (n, me)).wait_recv()
-        rcopy(fmeta_v, zf.at[o], msend.at[1, k], mrecv.at[1, o], (n, me)).wait_recv()
-    to_s2 = pltpu.make_async_copy(zi.at[:, :, pl.ds(0, HALF)], zis, local_sem.at[5])
-    to_s3 = pltpu.make_async_copy(zf, zfs, local_sem.at[6])
-    to_s2.start()
-    to_s3.start()
+        for i, (a, b) in enumerate(
+            ((flags_h, zflags.at[o]), (offs_h, zoffs.at[o]), (weights_h, zw.at[o]), (zfirst.at[o], zfirst.at[o]))
+        ):
+            rcopy(a, b, msend.at[i, k], mrecv.at[i, o], (n, me)).wait_recv()
+    to_smem = [
+        pltpu.make_async_copy(a, b, local_sem.at[17 + i])
+        for i, (a, b) in enumerate(((zoffs, zoffs_s), (zw, zw_s), (zfirst, zfirst_s)))
+    ]
+    for c in to_smem:
+        c.start()
 
     for w in (0, 1):
         zcopy(0, w).wait_recv()
@@ -305,20 +325,20 @@
     prepare(1)
     prepare(2)
 
-    to_s2.wait()
-    to_s3.wait()
-    first_down, first_up, first_far = zis[down, 0, 32], zis[up, 0, 32], zis[far, 0, 32]
+    for c in to_smem:
+        c.wait()
+    first_down, first_up, first_far = zfirst_s[down, 0, 0], zfirst_s[up, 0, 0], zfirst_s[far, 0, 0]
 
     total = jnp.zeros((1, CH), F32)
     bin_here = n * BINS + me
     for k in range(NIGHTS):
-        l = bin_here - zis[k, 0, 32]
+        l = bin_here - zfirst_s[k, 0, 0]
         valid = flag((l >= 0) & (l < BINS))
         lc = jnp.clip(l, 0, BINS - 1)
-        off = zis[k, 0, lc]
+        off = zoffs_s[k, 0, lc]
         for t in range(TAPS):
-            bits = (zi[k, :, pl.ds(HALF, CH)] >> (off + t)) & 1
-            total = total + (valid * zfs[k, 0, lc * 4 + t]) * (1.0 - bits.astype(F32))
+            bits = (zflags[k] >> (off + t)) & 1
+            total = total + (valid * zw_s[k, t, lc]) * (1.0 - bits.astype(F32))
     wt_ref[...] = total
 
     def wait_rows(k, _):
@@ -485,17 +505,13 @@
     visibilities, corrupted_sample_markers, antenna_gain_table, baseline_antennas, first_bin, tap_offsets, tap_weights,
     lst_delay, fringe_rate,
 ):
-    vis = visibilities.reshape(2, 4, SAMPLES, CH)
-    gains = antenna_gain_table.reshape(2, OWN_ANT, CH)
-    small = jnp.concatenate([tap_offsets.reshape(32), first_bin, jnp.zeros((95,), I32)])
-    imeta = jnp.concatenate([small, corrupted_sample_markers.reshape(CH)]).reshape(1, HALF + CH)
-    fmeta = tap_weights.reshape(1, HALF)
-    bas = jnp.concatenate([baseline_antennas.T.reshape(8), jnp.zeros((120,), I32)]).reshape(1, HALF)
-    fr8 = jnp.broadcast_to(jnp.tile(fringe_rate * (1.0 / (2.0 * math.pi)), 2)[:, None], (ROWS, WIDE))
+    vis = jnp.transpose(visibilities[:, 0], (0, 2, 1, 3))
+    gains = jnp.transpose(antenna_gain_table, (0, 2, 1, 3))
+    weights = jnp.transpose(tap_weights[0], (1, 0))
+    bas = jnp.transpose(baseline_antennas, (1, 0))
 
     vm = pl.BlockSpec(memory_space=pltpu.VMEM)
-    sm = pl.BlockSpec(memory_space=pltpu.SMEM)
-    hbm = pl.BlockSpec(memory_space=pl.ANY)
+    hbm = pl.BlockSpec(memory_space=pltpu.HBM)
     D = pltpu.SemaphoreType.DMA
     msg = (STAGES, BINS, ROWS, HALF)
     landed, wt = pl.pallas_call(
@@ -504,34 +520,42 @@
             jax.ShapeDtypeStruct((STAGES, DEVS, ROWS, WIDE), F32),
             jax.ShapeDtypeStruct((1, CH), F32),
         ),
-        in_specs=[hbm, hbm, vm, vm, vm, vm, sm, sm, sm],
+        in_specs=[hbm] * 9,
         out_specs=(vm, vm),
         scratch_shapes=[
-            pltpu.VMEM((2, 4, SAMPLES, CH), F32),
+            pltpu.SMEM((1, BINS), I32),
+            pltpu.SMEM((1,), I32),
+            pltpu.SMEM((TAPS, BINS), F32),
+            pltpu.SMEM((1, BINS), F32),
+            pltpu.SMEM((4,), F32),
+            pltpu.VMEM((2, SAMPLES, 4, CH), F32),
             pltpu.VMEM((SAMPLES, ROWS, CH), F32),
             pltpu.VMEM((STAGES, BINS, ROWS, WIDE), F32),
             pltpu.VMEM((STAGES, BINS, ROWS, WIDE), F32),
-            pltpu.VMEM((4, 2, OWN_ANT, GHALF), F32),
-            pltpu.VMEM((4, 2, OWN_ANT, GHALF), F32),
-            pltpu.VMEM((8, 1, HALF), I32),
-            pltpu.VMEM((8, 1, HALF), I32),
-            pltpu.SMEM((8, 1, HALF), I32),
-            pltpu.SMEM((8, 1, HALF), I32),
+            pltpu.VMEM((4, 2, OWN_ANT, 1, GHALF), F32),
+            pltpu.VMEM((4, 2, OWN_ANT, 1, GHALF), F32),
+            pltpu.VMEM((8, 2, 4), I32),
+            pltpu.VMEM((8, 2, 4), I32),
+            pltpu.SMEM((8, 2, 4), I32),
+            pltpu.SMEM((8, 2, 4), I32),
             pltpu.VMEM((8, 2, ROWS, GHALF), F32),
             pltpu.VMEM((8, 2, ROWS, GHALF), F32),
             pltpu.VMEM((8, 2, ROWS, GHALF), F32),
             pltpu.VMEM((8, 2, ROWS, GHALF), F32),
             pltpu.VMEM((2, ROWS, CH), F32),
             pltpu.VMEM((NIGHTS, 2, ROWS, WIDE), F32),
-            pltpu.VMEM((NIGHTS, 1, HALF + CH), I32),
-            pltpu.VMEM((NIGHTS, 1, HALF), F32),
+            pltpu.VMEM((NIGHTS, 1, CH), I32),
+            pltpu.VMEM((NIGHTS, 1, HALF), I32),
+            pltpu.VMEM((NIGHTS, 1, BINS), I32),
+            pltpu.VMEM((NIGHTS, TAPS, BINS), F32),
             pltpu.SMEM((NIGHTS, 1, HALF), I32),
-            pltpu.SMEM((NIGHTS, 1, HALF), F32),
+            pltpu.SMEM((NIGHTS, 1, BINS), I32),
+            pltpu.SMEM((NIGHTS, TAPS, BINS), F32),
         ]
         + [pltpu.VMEM(msg, F32)] * 8
         + [pltpu.VMEM(msg[1:], F32)] * 2
         + [
-            D((7,)), D((2, 4)), D((4,)), D((4,)), D((2, 8)), D((8,)), D((8,)), D((2, 4)), D((2, 4)),
+            D((20,)), D((2, 4)), D((4,)), D((4,)), D((2, 8)), D((8,)), D((8,)), D((4, 4)), D((4, 4)),
             D((8,)), D((8,)), D((8,)), D((8,)), D((STAGES + 1, 4)), D((STAGES + 1, 4)), D((4,)), D((4,)),
             D((STAGES,)), D((STAGES,)),
         ],
@@ -539,7 +563,7 @@
             collective_id=0, has_side_effects=True, vmem_limit_bytes=40 * 1024 * 1024
         ),
         name="exchange",
-    )(vis, gains, imeta, fmeta, bas, fr8, small, fmeta.reshape(HALF), lst_delay.reshape(BINS))
+    )(vis, gains, corrupted_sample_markers, tap_offsets, first_bin, weights, lst_delay, bas, fringe_rate)
 
     binned, weight_total = pl.pallas_call(
         final_kernel,

time: 53.2 us -> 48.5 us (0.912)
  other arithmetic: 2.82 us -> 0 us
  local copies, waits for them, and re-layouts: 3.88 us -> 2.7 us
    concatenate x2 -> x0, other arithmetic: 1.47 us -> none  [the longest x1 0.74 us: per_device(): jnp.concatenate([small, corrupted_sample_markers.reshape(CH)])]
    reshape x5 -> x0, local copies, waits for them, and re-layouts: 0.89 us -> none  [the longest x1 0.76 us: per_device(): baseline_antennas.T.reshape(8)]
    unnamed x1 -> x0, other arithmetic: 0.7 us -> none
    mul x1 -> x0, other arithmetic: 0.66 us -> none  [per_device(): fringe_rate * (1.0 / (2.0 * math.pi))]
    unnamed x7 -> x16, local copies, waits for them, and re-layouts: 2.73 us -> 2.7 us
where the time goes in v2:
time: 48.5 us; the launch traced here: 48.3 us
  Pallas kernels  44.3 us (91%)
  local copies, waits for them, and re-layouts  2.7 us (6%)
  between operations  1.34 us (3%)
    pallas_call x1, Pallas kernels, per_device(): pl.pallas_call(comm_kernel, out_shape=(jax.ShapeDtypeStruct((STAGES, DEVS...  43 us
    unnamed x16, local copies, waits for them, and re-layouts  2.7 us
    pallas_call x1, Pallas kernels, per_device(): pl.pallas_call(final_kernel, out_shape=(jax.ShapeDtypeStruct((2, 4 * DEVS...  1.22 us

profile of v2, /device:TPU:1, one launch (start us, length us, event | category | flops | bytes accessed | tf_op | source)
XLA Modules:
  0.0 48.3 jit_solution(9364744577999082152)
XLA Ops:
  1.3 0.0 copy-start.4
  1.3 0.0 copy-start.6
  1.3 0.0 copy-start.7
  1.3 0.0 copy-start.2
  1.3 0.0 copy-start.3
  1.3 0.0 copy-start.5
  1.3 0.6 %copy-done.4 = s32[4,2]{0,1:T(2,128)S(1)} copy-done((s32[4,2]{0,1:T(2,128)S(1)}, s32[4,2]{0,1:T(2,128)}, u32[]{:S(2)}) %copy-start.4) | copy-done | bytes 56
  2.0 0.0 copy-done.6
  2.0 0.0 copy-done.7
  2.0 0.0 copy-done.2
  2.0 0.0 copy-done.3
  2.0 0.0 copy-done.5
  2.0 0.0 copy-start
  2.0 1.1 %copy-done = f32[2,1,4,30,768]{4,2,3,1,0:T(4,128)S(1)} copy-done((f32[2,1,4,30,768]{4,2,3,1,0:T(4,128)S(1)}, f32[2,1,4,30,768]{4,2,3,1,0:T(4,128)}, u32[]{:S(2)}) %copy-start) | copy-done | bytes 737304
  3.1 0.0 copy-start.1
  3.1 0.9 %copy-done.1 = f32[2,1,11,768]{3,1,2,0:T(1,128)S(1)} copy-done((f32[2,1,11,768]{3,1,2,0:T(1,128)S(1)}, f32[2,1,11,768]{3,1,2,0:T(1,128)}, u32[]{:S(2)}) %copy-start.1) | copy-done | bytes 67608
  4.0 43.0 %exchange.1 = (f32[3,32,8,256]{3,2,1,0:T(8,128)S(1)}, f32[1,768]{1,0:T(1,128)S(1)}) custom-call(f32[2,30,4,768]{3,2,1,0:T(4,128)S(1)} %bitcast.11, f32[2,11,1,768]{3,2,1,0:T(1,128)S(1)} %bitcast.12, s32[1,768]{1,0:T(1,128)S(1)} %copy-done.2, s32[1,32]{1,0:T(1,128)S(1)} %copy-done.5, s32[1]{0:T(128)S(6)} %copy.12.first_h, f32[4,32]{1,0:T(4,128)S(1)} %bitcast.13, ...), custom_call_target="tpu_custom_call" | custom-call | tf_op jit(solution)/shard_map/exchange/pallas_call | solution.py:517
  47.1 1.2 %assemble.1 = (f32[2,128,768]{2,1,0:T(8,128)}, f32[1,768]{1,0:T(1,128)}) custom-call(f32[3,32,8,256]{3,2,1,0:T(8,128)S(1)} %get-tuple-element.6.landed, f32[1,768]{1,0:T(1,128)S(1)} %get-tuple-element.7.wt), custom_call_target="tpu_custom_call" | custom-call | tf_op jit(solution)/shard_map/assemble/pallas_call | solution.py:568
Async XLA Ops:
  1.3 0.7 %copy-start.4 = (s32[4,2]{0,1:T(2,128)S(1)}, s32[4,2]{0,1:T(2,128)}, u32[]{:S(2)}) copy-start(s32[4,2]{0,1:T(2,128)} %param.12) | copy-start | bytes 100
  1.3 0.7 %copy-start.6 = (f32[1,32]{1,0:T(1,128)S(1)}, f32[1,32]{1,0:T(1,128)}, u32[]{:S(2)}) copy-start(f32[1,32]{1,0:T(1,128)} %delay_h.1) | copy-start | bytes 388
  1.3 0.7 %copy-start.7 = (f32[4]{0:T(128)S(1)}, f32[4]{0:T(128)}, u32[]{:S(2)}) copy-start(f32[4]{0:T(128)} %rate_h.1) | copy-start | bytes 52
  1.3 0.7 %copy-start.2 = (s32[1,768]{1,0:T(1,128)S(1)}, s32[1,768]{1,0:T(1,128)}, u32[]{:S(2)}) copy-start(s32[1,768]{1,0:T(1,128)} %flags_h.1) | copy-start | bytes 9220
  1.3 0.7 %copy-start.3 = (f32[1,32,4]{1,2,0:T(4,128)S(1)}, f32[1,32,4]{1,2,0:T(4,128)}, u32[]{:S(2)}) copy-start(f32[1,32,4]{1,2,0:T(4,128)} %param.15) | copy-start | bytes 1540
  1.3 0.7 %copy-start.5 = (s32[1,32]{1,0:T(1,128)S(1)}, s32[1,32]{1,0:T(1,128)}, u32[]{:S(2)}) copy-start(s32[1,32]{1,0:T(1,128)} %offs_h.1) | copy-start | bytes 388
  2.0 1.1 %copy-start = (f32[2,1,4,30,768]{4,2,3,1,0:T(4,128)S(1)}, f32[2,1,4,30,768]{4,2,3,1,0:T(4,128)}, u32[]{:S(2)}) copy-start(f32[2,1,4,30,768]{4,2,3,1,0:T(4,128)} %param.9) | copy-start | bytes 2211844
  3.1 0.9 %copy-start.1 = (f32[2,1,11,768]{3,1,2,0:T(1,128)S(1)}, f32[2,1,11,768]{3,1,2,0:T(1,128)}, u32[]{:S(2)}) copy-start(f32[2,1,11,768]{3,1,2,0:T(1,128)} %param.11) | copy-start | bytes 202756

commit v3 on v2

--- a/solution.py
+++ b/solution.py
@@ -57,8 +57,8 @@
 
 def comm_kernel(
     vis, gains, flags_h, offs_h, first_h, weights_h, delay_h, bas_h, rate_h,
-    landed, wt_ref,
-    offs_s, first_s, weights_s, delay_s, rate_s, V, UV, Y, S, gy, gx, bx_v, by_v, bx_s, by_s, m0, m1, c0, c1, G, GZ,
+    out_ref, wt_ref,
+    offs_s, first_s, weights_s, delay_s, rate_s, V, UV, Y, Y2, S, landed, gy, gx, bx_v, by_v, bx_s, by_s, m0, m1, c0, c1, G, GZ,
     zflags, zfirst, zoffs, zw, zfirst_s, zoffs_s, zw_s, s1p, s1n, s2p, s2n, r1p, r1n, r2p, r2n, r3p, r3n,
     local_sem, gsend, gyr, gxr, bsend, bxr, byr, msend, mrecv,
     send0, send1, recv0, recv1, zsend, zrecv, gzs, gzr, asend, arecv,
@@ -77,7 +77,12 @@
             src_ref=src, dst_ref=dst, send_sem=ss, recv_sem=rs, device_id=dev, device_id_type=MESH
         )
 
-    load_vis = pltpu.make_async_copy(vis, V, local_sem.at[0])
+    load_vis = [
+        pltpu.make_async_copy(
+            vis.at[:, :, :, pl.ds(st * WIDE, WIDE)], V.at[:, :, :, pl.ds(st * WIDE, WIDE)], local_sem.at[20 + st]
+        )
+        for st in range(STAGES)
+    ]
     own_gy = pltpu.make_async_copy(gains.at[:, :, :, pl.ds(0, GHALF)], gy.at[y], local_sem.at[1])
     own_gx = pltpu.make_async_copy(gains.at[:, :, :, pl.ds(GHALF, GHALF)], gx.at[x], local_sem.at[2])
     small = [
@@ -90,22 +95,22 @@
             )
         )
     ]
-    for c in (*small, load_vis, own_gy, own_gx):
+    for c in (*small, *load_vis, own_gy, own_gx):
         c.start()
 
     barrier = pltpu.get_barrier_semaphore()
 
-    def greet_z(k, _):
-        pl.semaphore_signal(barrier, inc=1, device_id=(lax.rem(n + k, 4), me), device_id_type=MESH)
-        return _
-
-    def greet_bl(k, _):
-        pl.semaphore_signal(barrier, inc=1, device_id=(n, lax.rem(me + k, DEVS)), device_id_type=MESH)
-        return _
-
-    lax.fori_loop(1, NIGHTS, greet_z, 0)
-    lax.fori_loop(1, DEVS, greet_bl, 0)
-    pl.semaphore_wait(barrier, NIGHTS - 1 + DEVS - 1)
+    def greet(device):
+        pl.semaphore_signal(barrier, inc=1, device_id=device, device_id_type=MESH)
+
+    for k in (1, 2, 3):
+        greet((lax.rem(n + k, 4), me))
+    greet((n, bl_of(y, x, 1 - core)))
+    for k in (1, 2, 3):
+        for cc in range(2):
+            greet((n, bl_of(y, lax.rem(x + k, 4), cc)))
+            greet((n, bl_of(lax.rem(y + k, 4), x, cc)))
+    pl.semaphore_wait(barrier, 16)
 
     def gain_a(k):
         ty = lax.rem(y + k, 4)
@@ -115,10 +120,6 @@
             rcopy(gains.at[:, :, :, pl.ds(GHALF, GHALF)], gx.at[x], gsend.at[1, k], gxr.at[x], (n, bl_of(y, tx, core))),
         )
 
-    for k in (1, 3, 2):
-        for c in gain_a(k):
-            c.start()
-
     def slot_dev(k, own):
         s = lax.rem(own + k, 8)
         return s, s // 2, lax.rem(s, 2)
@@ -139,6 +140,9 @@
         return _
 
     lax.fori_loop(1, 8, start_bas, 0)
+    for k in (1, 3, 2):
+        for c in gain_a(k):
+            c.start()
 
     for c in small:
         c.wait()
@@ -157,10 +161,6 @@
             )
         ]
 
-    for k in (1, 3, 2):
-        for c in meta(k):
-            c.start()
-
     def shift_of(f, night, e):
         return (lax.shift_right_logical(f, 5) + jnp.where(e < (f & 31), 1, 0) - night) & 3
 
@@ -173,10 +173,9 @@
         which < 2, jnp.where(which == 0, rate_s[0], rate_s[1]), jnp.where(which == 2, rate_s[2], rate_s[3])
     ) * (1.0 / (2.0 * math.pi))
 
-    load_vis.wait()
-
     def prepare(st):
         at = st * WIDE
+        load_vis[st].wait()
 
         def per_sample(t, _):
             bits = (zflags[n, :, pl.ds(at, WIDE)] >> t) & 1
@@ -248,6 +247,10 @@
     zcopy(0, 2).start()
     zcopy(0, 3).start()
 
+    for k in (1, 3, 2):
+        for c in meta(k):
+            c.start()
+
     def wait_bas(k, _):
         sx = lax.rem(x * 2 + core + k, 8)
         sy = lax.rem(y * 2 + core + k, 8)
@@ -325,22 +328,6 @@
     prepare(1)
     prepare(2)
 
-    for c in to_smem:
-        c.wait()
-    first_down, first_up, first_far = zfirst_s[down, 0, 0], zfirst_s[up, 0, 0], zfirst_s[far, 0, 0]
-
-    total = jnp.zeros((1, CH), F32)
-    bin_here = n * BINS + me
-    for k in range(NIGHTS):
-        l = bin_here - zfirst_s[k, 0, 0]
-        valid = flag((l >= 0) & (l < BINS))
-        lc = jnp.clip(l, 0, BINS - 1)
-        off = zoffs_s[k, 0, lc]
-        for t in range(TAPS):
-            bits = (zflags[k] >> (off + t)) & 1
-            total = total + (valid * zw_s[k, t, lc]) * (1.0 - bits.astype(F32))
-    wt_ref[...] = total
-
     def wait_rows(k, _):
         sx = lax.rem(x * 2 + core + k, 8)
         sy = lax.rem(y * 2 + core + k, 8)
@@ -367,40 +354,28 @@
     for k in (1, 3, 2):
         gz(k).start()
 
-    for st in (1, 2):
+    def with_gain(st, build):
         gr, gs = G[0, :, pl.ds(st * WIDE, WIDE)], G[1, :, pl.ds(st * WIDE, WIDE)]
 
-        def apply(e, _, st=st, gr=gr, gs=gs):
+        def per_bin(e, _):
             v = Y[st, e]
             v = gr * v + gs * swap4(v)
             Y[st, e] = v
-            s = shift_of(first, n, e)
-            a, b = v[:, :HALF], v[:, HALF:]
-            two = flag(s == 2)
-            s1p[st, e] = two * a + flag(s == 1) * b
-            s1n[st, e] = two * b + flag(s == 3) * a
+            if build:
+                first_message(st, e, shift_of(first, n, e), v[:, :HALF], v[:, HALF:])
             return _
 
-        lax.fori_loop(0, BINS, apply, 0)
-        zcopy(st, 0).start()
-        zcopy(st, 1).start()
-
-    for st in (1, 2):
-        zcopy(st, 0).wait_recv()
-        zcopy(st, 1).wait_recv()
-
-        def second(e, _, st=st):
-            s = shift_of(first, n, e)
-            s2p[st, e] = flag(s == 1) * Y[st, e, :, lo] + flag(shift_of(first_down, down, e) == 2) * r1p[st, e]
-            s2n[st, e] = flag(s == 3) * Y[st, e, :, hi] + flag(shift_of(first_up, up, e) == 2) * r1n[st, e]
-            return _
-
-        lax.fori_loop(0, BINS, second, 0)
-        zcopy(st, 2).start()
-        zcopy(st, 3).start()
+        lax.fori_loop(0, BINS, per_bin, 0)
+
+    def first_message(st, e, s, a, b):
+        two = flag(s == 2)
+        s1p[st, e] = two * a + flag(s == 1) * b
+        s1n[st, e] = two * b + flag(s == 3) * a
 
     def bin_copy(st, k):
         t = lax.rem(me + k, DEVS)
+        if st == 2:
+            return rcopy(Y.at[2, t], Y2.at[me], asend.at[2], arecv.at[2], (n, t))
         return rcopy(S.at[st, t], landed.at[st, me], asend.at[st], arecv.at[st], (n, t))
 
     def send_bins(st):
@@ -409,7 +384,49 @@
             return _
 
         lax.fori_loop(1, DEVS, go, 0)
-        landed[st, me] = S[st, me]
+        if st == 2:
+            Y2[me] = Y[2, me]
+        else:
+            landed[st, me] = S[st, me]
+
+    def all_bins(st):
+        part = pl.ds(0, DEVS - 1)
+        if st == 2:
+            return rcopy(Y.at[2, part], Y2.at[part], asend.at[2], arecv.at[2], (n, me))
+        return rcopy(S.at[st, part], landed.at[st, part], asend.at[st], arecv.at[st], (n, me))
+
+    with_gain(1, True)
+    zcopy(1, 0).start()
+    zcopy(1, 1).start()
+    with_gain(2, False)
+    send_bins(2)
+
+    for c in to_smem:
+        c.wait()
+    first_down, first_up, first_far = zfirst_s[down, 0, 0], zfirst_s[up, 0, 0], zfirst_s[far, 0, 0]
+    total = jnp.zeros((1, CH), F32)
+    bin_here = n * BINS + me
+    for k in range(NIGHTS):
+        l = bin_here - zfirst_s[k, 0, 0]
+        valid = flag((l >= 0) & (l < BINS))
+        lc = jnp.clip(l, 0, BINS - 1)
+        off = zoffs_s[k, 0, lc]
+        for t in range(TAPS):
+            bits = (zflags[k] >> (off + t)) & 1
+            total = total + (valid * zw_s[k, t, lc]) * (1.0 - bits.astype(F32))
+    wt_ref[...] = total
+    scale = 1.0 / jnp.maximum(total, 0.5)
+
+    def put(st, k, a, b, inv):
+        a, b = a * inv, b * inv
+        low = row < 4
+        at = pl.multiple_of(k * 8, 8)
+        cols = pl.ds(st * WIDE, WIDE)
+        out_ref[0, pl.ds(at, 8), cols] = jnp.where(low, a, swap4(b))
+        out_ref[1, pl.ds(at, 8), cols] = jnp.where(low, swap4(a), b)
+
+    def scale_of(st):
+        return jnp.broadcast_to(scale[:, st * WIDE : (st + 1) * WIDE], (ROWS, WIDE))
 
     for k in (1, 2, 3):
         o = lax.rem(n + k, 4)
@@ -439,20 +456,87 @@
     lax.fori_loop(0, BINS, combine0, 0)
     send_bins(0)
 
-    for st in (1, 2):
-        zcopy(st, 2).wait_recv()
-        zcopy(st, 3).wait_recv()
-
-        def combine(e, _, st=st):
-            here = flag(shift_of(first, n, e) == 0)
-            from_down = flag(shift_of(first_down, down, e) == 1)
-            from_up = flag(shift_of(first_up, up, e) == 3)
-            S[st, e, :, lo] = here * Y[st, e, :, lo] + from_up * r1n[st, e] + r2p[st, e]
-            S[st, e, :, hi] = here * Y[st, e, :, hi] + from_down * r1p[st, e] + r2n[st, e]
+    def second_message(st, i, e, a, b):
+        s = shift_of(first, n, e)
+        s2p[st, i] = flag(s == 1) * a + flag(shift_of(first_down, down, e) == 2) * r1p[st, i]
+        s2n[st, i] = flag(s == 3) * b + flag(shift_of(first_up, up, e) == 2) * r1n[st, i]
+
+    def merged(st, i, e, a, b):
+        here = flag(shift_of(first, n, e) == 0)
+        from_down = flag(shift_of(first_down, down, e) == 1)
+        from_up = flag(shift_of(first_up, up, e) == 3)
+        return (
+            here * a + from_up * r1n[st, i] + r2p[st, i],
+            here * b + from_down * r1p[st, i] + r2n[st, i],
+        )
+
+    zcopy(1, 0).wait_recv()
+    zcopy(1, 1).wait_recv()
+
+    def second1(e, _):
+        second_message(1, e, e, Y[1, e, :, lo], Y[1, e, :, hi])
+        return _
+
+    lax.fori_loop(0, BINS, second1, 0)
+    zcopy(1, 2).start()
+    zcopy(1, 3).start()
+
+    all_bins(2).wait_recv()
+
+    def first2(d, _):
+        first_message(2, d, shift_of(first, n, me), Y2[d, :, lo], Y2[d, :, hi])
+        return _
+
+    lax.fori_loop(0, DEVS, first2, 0)
+    zcopy(2, 0).start()
+    zcopy(2, 1).start()
+
+    zcopy(1, 2).wait_recv()
+    zcopy(1, 3).wait_recv()
+
+    def combine1(e, _):
+        a, b = merged(1, e, e, Y[1, e, :, lo], Y[1, e, :, hi])
+        S[1, e, :, lo] = a
+        S[1, e, :, hi] = b
+        return _
+
+    lax.fori_loop(0, BINS, combine1, 0)
+    send_bins(1)
+
+    zcopy(2, 0).wait_recv()
+    zcopy(2, 1).wait_recv()
+
+    def second2(d, _):
+        second_message(2, d, me, Y2[d, :, lo], Y2[d, :, hi])
+        return _
+
+    lax.fori_loop(0, DEVS, second2, 0)
+    zcopy(2, 2).start()
+    zcopy(2, 3).start()
+
+    for st in (0, 1):
+        all_bins(st).wait_recv()
+        inv = scale_of(st)
+
+        def assemble(k, _, st=st, inv=inv):
+            put(st, k, landed[st, 2 * k], landed[st, 2 * k + 1], inv)
             return _
 
-        lax.fori_loop(0, BINS, combine, 0)
-        send_bins(st)
+        lax.fori_loop(0, DEVS // 2, assemble, 0)
+
+    zcopy(2, 2).wait_recv()
+    zcopy(2, 3).wait_recv()
+    inv2 = scale_of(2)
+
+    def finish(k, _):
+        pair = []
+        for d in (2 * k, 2 * k + 1):
+            a, b = merged(2, d, me, Y2[d, :, lo], Y2[d, :, hi])
+            pair.append(jnp.concatenate([a, b], axis=1))
+        put(2, k, pair[0], pair[1], inv2)
+        return _
+
+    lax.fori_loop(0, DEVS // 2, finish, 0)
 
     for k in (1, 2, 3):
         for c in gain_a(k):
@@ -475,30 +559,7 @@
     for w in (0, 1):
         forward(w).wait_send()
     for st in range(STAGES):
-        whole = rcopy(
-            S.at[st, pl.ds(0, DEVS - 1)], landed.at[st, pl.ds(0, DEVS - 1)], asend.at[st], arecv.at[st], (n, me)
-        )
-        whole.wait_send()
-        whole.wait_recv()
-
-
-def final_kernel(landed, wt, out, wt_out):
-    row = lax.broadcasted_iota(I32, (ROWS, WIDE), 0)
-    low = row < 4
-    wt_out[...] = wt[...]
-    for st in range(STAGES):
-        cols = pl.ds(st * WIDE, WIDE)
-        inv = jnp.broadcast_to(1.0 / jnp.maximum(wt[:, cols], 0.5), (ROWS, WIDE))
-
-        def pair(k, _, st=st, cols=cols, inv=inv):
-            a = landed[st, 2 * k] * inv
-            b = landed[st, 2 * k + 1] * inv
-            at = pl.multiple_of(k * 8, 8)
-            out[0, pl.ds(at, 8), cols] = jnp.where(low, a, swap4(b))
-            out[1, pl.ds(at, 8), cols] = jnp.where(low, swap4(a), b)
-            return _
-
-        lax.fori_loop(0, DEVS // 2, pair, 0)
+        all_bins(st).wait_send()
 
 
 def per_device(
@@ -510,14 +571,17 @@
     weights = jnp.transpose(tap_weights[0], (1, 0))
     bas = jnp.transpose(baseline_antennas, (1, 0))
 
+    def held(a):
+        return pltpu.with_memory_space_constraint(a, pltpu.HBM)
+
     vm = pl.BlockSpec(memory_space=pltpu.VMEM)
     hbm = pl.BlockSpec(memory_space=pltpu.HBM)
     D = pltpu.SemaphoreType.DMA
     msg = (STAGES, BINS, ROWS, HALF)
-    landed, wt = pl.pallas_call(
+    binned, weight_total = pl.pallas_call(
         comm_kernel,
         out_shape=(
-            jax.ShapeDtypeStruct((STAGES, DEVS, ROWS, WIDE), F32),
+            pltpu.VMEM((2, 4 * DEVS, CH), F32),
             jax.ShapeDtypeStruct((1, CH), F32),
         ),
         in_specs=[hbm] * 9,
@@ -531,7 +595,9 @@
             pltpu.VMEM((2, SAMPLES, 4, CH), F32),
             pltpu.VMEM((SAMPLES, ROWS, CH), F32),
             pltpu.VMEM((STAGES, BINS, ROWS, WIDE), F32),
-            pltpu.VMEM((STAGES, BINS, ROWS, WIDE), F32),
+            pltpu.VMEM((DEVS, ROWS, WIDE), F32),
+            pltpu.VMEM((2, BINS, ROWS, WIDE), F32),
+            pltpu.VMEM((2, DEVS, ROWS, WIDE), F32),
             pltpu.VMEM((4, 2, OWN_ANT, 1, GHALF), F32),
             pltpu.VMEM((4, 2, OWN_ANT, 1, GHALF), F32),
             pltpu.VMEM((8, 2, 4), I32),
@@ -555,24 +621,18 @@
         + [pltpu.VMEM(msg, F32)] * 8
         + [pltpu.VMEM(msg[1:], F32)] * 2
         + [
-            D((20,)), D((2, 4)), D((4,)), D((4,)), D((2, 8)), D((8,)), D((8,)), D((4, 4)), D((4, 4)),
+            D((23,)), D((2, 4)), D((4,)), D((4,)), D((2, 8)), D((8,)), D((8,)), D((4, 4)), D((4, 4)),
             D((8,)), D((8,)), D((8,)), D((8,)), D((STAGES + 1, 4)), D((STAGES + 1, 4)), D((4,)), D((4,)),
             D((STAGES,)), D((STAGES,)),
         ],
         compiler_params=pltpu.CompilerParams(
-            collective_id=0, has_side_effects=True, vmem_limit_bytes=40 * 1024 * 1024
+            collective_id=0, has_side_effects=True, vmem_limit_bytes=48 * 1024 * 1024
         ),
         name="exchange",
-    )(vis, gains, corrupted_sample_markers, tap_offsets, first_bin, weights, lst_delay, bas, fringe_rate)
-
-    binned, weight_total = pl.pallas_call(
-        final_kernel,
-        out_shape=(jax.ShapeDtypeStruct((2, 4 * DEVS, CH), F32), jax.ShapeDtypeStruct((1, CH), F32)),
-        in_specs=[vm, vm],
-        out_specs=(vm, vm),
-        compiler_params=pltpu.CompilerParams(vmem_limit_bytes=16 * 1024 * 1024),
-        name="assemble",
-    )(landed, wt)
+    )(
+        held(vis), held(gains), held(corrupted_sample_markers), held(tap_offsets), first_bin, held(weights),
+        held(lst_delay), held(bas), held(fringe_rate),
+    )
     return binned.reshape(2, 1, 4 * DEVS, CH), weight_total
 
 

time: 48.5 us -> 43.3 us (0.89)
  Pallas kernels: 44.3 us -> 40.4 us
  local copies, waits for them, and re-layouts: 2.7 us -> 1.46 us
    pallas_call x2 -> x1, Pallas kernels: 44.3 us -> 40.4 us  [per_device(): pl.pallas_call(comm_kernel, out_shape=(pltpu.VMEM((2, 4 * DEVS, CH), F32)...]
    unnamed x16 -> x2, local copies, waits for them, and re-layouts: 2.7 us -> 1.46 us
where the time goes in v3:
time: 43.3 us; the launch traced here: 43.2 us
  Pallas kernels  40.4 us (93%)
  local copies, waits for them, and re-layouts  1.46 us (3%)
  between operations  1.29 us (3%)
    pallas_call x1, Pallas kernels, per_device(): pl.pallas_call(comm_kernel, out_shape=(pltpu.VMEM((2, 4 * DEVS, CH), F32)...  40.4 us
    unnamed x2, local copies, waits for them, and re-layouts  1.46 us

profile of v3, /device:TPU:1, one launch (start us, length us, event | category | flops | bytes accessed | tf_op | source)
XLA Modules:
  0.0 43.2 jit_solution(11738185833872912072)
XLA Ops:
  1.3 40.4 %exchange.1 = (f32[2,128,768]{2,1,0:T(8,128)S(1)}, f32[1,768]{1,0:T(1,128)S(1)}) custom-call(f32[2,30,4,768]{3,2,1,0:T(4,128)} %bitcast.12, f32[2,11,1,768]{3,2,1,0:T(1,128)} %bitcast.13, s32[1,768]{1,0:T(1,128)} %flags_h.1, s32[1,32]{1,0:T(1,128)} %offs_h.1, s32[1]{0:T(128)S(6)} %copy.15.first_h, f32[4,32]{1,0:T(4,128)} %bitcast.14, f32[1,32]{1,0:T(1,128)} %delay_h.1, ...), custom_call_target="tpu_custom_call" | custom-call | tf_op jit(solution)/shard_map/exchange/pallas_call | solution.py:581
  41.7 0.9 %copy.14 = f32[2,1,128,768]{3,2,1,0:T(8,128)} copy(f32[2,1,128,768]{3,2,1,0:T(8,128)S(1)} %bitcast.11) | data formatting | bytes 1572864
  42.6 0.6 %copy.16 = f32[1,768]{1,0:T(1,128)} copy(f32[1,768]{1,0:T(1,128)S(1)} %get-tuple-element.13) | data formatting | bytes 6144

commit v4 on v0

v4 whole, which is shorter than its diff:
```python
import functools
import math

import jax
import jax.numpy as jnp
import numpy as np
from jax import lax
from jax.experimental import pallas as pl
from jax.experimental.pallas import tpu as pltpu
from jax.sharding import PartitionSpec as P

MESH = pl.DeviceIdType.MESH
F32 = jnp.float32
I32 = jnp.int32

NIGHTS = 4
DEVS = 32
BINS = 32
ROWS = 8
CH = 768
SAMPLES = 30
TAPS = 4
OWN_ANT = 11
STAGES = 3
WIDE = 256
HALF = 128
SOON = 128
LATER = 256
EARLY = 512
HB = 16


def _fit(kind, terms):
    k = np.arange(200)
    u = 0.125 * (1 + np.cos(np.pi * (k + 0.5) / 200))
    r = np.sqrt(u)
    y = np.sin(2 * np.pi * r) / r if kind == "sin" else np.cos(2 * np.pi * r)
    cheb = np.polynomial.chebyshev.Chebyshev.fit(u, y, terms - 1, domain=[0, 0.25])
    return [float(v) for v in cheb.convert(kind=np.polynomial.Polynomial).coef]


SIN_C = _fit("sin", 8)
COS_C = _fit("cos", 8)


def horner(coef, u):
    acc = jnp.full_like(u, coef[-1])
    for c in coef[-2::-1]:
        acc = acc * u + c
    return acc


def swap4(v):
    return pltpu.roll(v, 4, 0)


def flag(cond):
    return jnp.where(cond, jnp.float32(1.0), jnp.float32(0.0))


def comm_kernel(
    vis, gains, flags_h, offs_h, first_h, weights_h, delay_h, bas_h, rate_h,
    out_ref, wt_ref,
    offs_s, first_s, weights_s, delay_s, rate_s, V, UV, Y, Y2, S, landed, gyu, gxu, gyl, gxl, bx_v, by_v, bx_s, by_s,
    m0, m1, c0, c1, q0, q1, d0, d1, G, GP, GZ,
    zflags, zfirst, zoffs, zw, zfirst_s, zoffs_s, zw_s, s1p, s1n, s2p, s2n, r1p, r1n, r2p, r2n, r3p, r3n,
    local_sem, gsend, grecv, bsend, bxr, byr, msend, mrecv,
    rsend, rrecv, zsend, zrecv, gzs, gzr, asend, arecv,
):
    n = lax.axis_index("night")
    me = lax.axis_index("bl")
    core = lax.rem(me, 2)
    x = lax.rem(me // 2, 4)
    y = me // 8

    def bl_of(yy, xx, cc):
        return (yy * 4 + xx) * 2 + cc

    def rcopy(src, dst, ss, rs, dev):
        return pltpu.make_async_remote_copy(
            src_ref=src, dst_ref=dst, send_sem=ss, recv_sem=rs, device_id=dev, device_id_type=MESH
        )

    def loop(count, body, unroll=4, start=0):
        def step(i, c):
            body(i)
            return c

        lax.fori_loop(start, count, step, 0, unroll=unroll)

    load_vis = [
        pltpu.make_async_copy(
            vis.at[:, :, :, pl.ds(st * WIDE, WIDE)], V.at[:, :, :, pl.ds(st * WIDE, WIDE)], local_sem.at[st]
        )
        for st in range(STAGES)
    ]

    def table(which, late):
        begin = ((512, 640), (0, 256))[late][which]
        return gains.at[:, :, :, pl.ds(begin, LATER if late else SOON)], ((gyu, gxu), (gyl, gxl))[late][which]

    own_gains = []
    for late in (0, 1):
        for which in (0, 1):
            src, dst = table(which, late)
            own_gains.append(pltpu.make_async_copy(src, dst.at[(y, x)[which]], local_sem.at[3 + 2 * late + which]))
    small = [
        pltpu.make_async_copy(a, b, local_sem.at[7 + i])
        for i, (a, b) in enumerate(
            (
                (first_h, first_s), (offs_h, offs_s), (weights_h, weights_s), (delay_h, delay_s), (rate_h, rate_s),
                (flags_h, zflags.at[n]), (offs_h, zoffs.at[n]), (weights_h, zw.at[n]),
                (bas_h, bx_v.at[x * 2 + core]), (bas_h, by_v.at[y * 2 + core]),
            )
        )
    ]
    for c in (load_vis[0], *small[:6]):
        c.start()

    barrier = pltpu.get_barrier_semaphore()

    def greet(device):
        pl.semaphore_signal(barrier, inc=1, device_id=device, device_id_type=MESH)

    for k in (1, 2, 3):
        greet((lax.rem(n + k, 4), me))
    greet((n, bl_of(y, x, 1 - core)))
    for k in (1, 2, 3):
        for cc in range(2):
            greet((n, bl_of(y, lax.rem(x + k, 4), cc)))
            greet((n, bl_of(lax.rem(y + k, 4), x, cc)))
    for c in (*small[6:], *own_gains, *load_vis[1:]):
        c.start()

    lane = lax.broadcasted_iota(I32, (ROWS, WIDE), 1).astype(F32)
    row = lax.broadcasted_iota(I32, (ROWS, WIDE), 0)
    sign = jnp.where(row < 4, jnp.float32(-1.0), jnp.float32(1.0))
    for c in small[:6]:
        c.wait()
    first = first_s[0]
    zfirst[n] = jnp.full((1, HALF), first, I32)
    which_row = row & 3
    rates = jnp.where(
        which_row < 2,
        jnp.where(which_row == 0, rate_s[0], rate_s[1]),
        jnp.where(which_row == 2, rate_s[2], rate_s[3]),
    ) * (1.0 / (2.0 * math.pi))

    def samples(st):
        at = st * WIDE
        load_vis[st].wait()

        def per_sample(t):
            bits = (zflags[n, :, pl.ds(at, WIDE)] >> t) & 1
            both = jnp.concatenate([V[0, t, :, pl.ds(at, WIDE)], V[1, t, :, pl.ds(at, WIDE)]], axis=0)
            UV[t, :, pl.ds(at, WIDE)] = both * (1.0 - bits.astype(F32))

        loop(SAMPLES, per_sample, unroll=5)

    def shift_of(f, night, e):
        return (lax.shift_right_logical(f, 5) + jnp.where(e < (f & 31), 1, 0) - night) & 3

    def phases(st):
        return rates * (1.0 + (lane + float(st * WIDE)) * (1.0 / CH))

    def turned(st, rate, e):
        at = st * WIDE
        l = (e - first) & 31
        off = offs_s[0, l]
        acc = weights_s[0, l] * UV[off, :, pl.ds(at, WIDE)]
        for k in range(1, TAPS):
            acc = acc + weights_s[k, l] * UV[off + k, :, pl.ds(at, WIDE)]
        turns = rate * delay_s[0, l]
        r = turns - jnp.floor(turns + 0.5)
        u = r * r
        return horner(COS_C, u) * acc + (horner(SIN_C, u) * (r * sign)) * swap4(acc)

    up = lax.rem(n + 1, 4)
    down = lax.rem(n + 3, 4)
    far = lax.rem(n + 2, 4)

    def zcopy(st, which, h):
        src = (s1p, s1n, s2p, s2n)[which].at[st, pl.ds(h * HB, HB)]
        dst = (r1p, r1n, r2p, r2n)[which].at[st, pl.ds(h * HB, HB)]
        to = up if which % 2 == 0 else down
        return rcopy(src, dst, zsend.at[st, which, h], zrecv.at[st, which, h], (to, me))

    def forward(st, which, h):
        src, dst = ((r1p, r3p), (r1n, r3n))[which]
        part = pl.ds(h * HB, HB)
        to = (up, down)[which]
        return rcopy(
            src.at[st, part], dst.at[st, part], zsend.at[STAGES + st, which, h], zrecv.at[STAGES + st, which, h], (to, me)
        )

    lo = pl.ds(0, HALF)
    hi = pl.ds(HALF, HALF)

    def first_message(st, i, s, a, b):
        two = flag(s == 2)
        s1p[st, i] = two * a + flag(s == 1) * b
        s1n[st, i] = two * b + flag(s == 3) * a

    def second_message(st, i, e, a, b):
        s = shift_of(first, n, e)
        s2p[st, i] = flag(s == 1) * a + flag(shift_of(first_down, down, e) == 2) * r1p[st, i]
        s2n[st, i] = flag(s == 3) * b + flag(shift_of(first_up, up, e) == 2) * r1n[st, i]

    def early(st):
        samples(st)
        rate = phases(st)

        def per_bin(e):
            v = turned(st, rate, e)
            Y[st, e] = v
            a, b = v[:, :HALF], v[:, HALF:]
            s = shift_of(first, n, e)
            first_message(st, e, s, a, b)
            s2p[st, e] = flag(s == 1) * a
            s2n[st, e] = flag(s == 3) * b

        loop(BINS, per_bin)

    def start_early(st, message):
        for h in (0, 1):
            for w in (0, 1):
                zcopy(st, 2 * message + w, h).start()

    early(0)
    pl.semaphore_wait(barrier, 16)
    start_early(0, 0)
    start_early(0, 1)
    for c in (*small[6:], *own_gains):
        c.wait()

    def gain_a(which, late, k):
        _, tab = table(which, late)
        mine = (y, x)[which]
        to = bl_of(lax.rem(y + k, 4), x, core) if which == 0 else bl_of(y, lax.rem(x + k, 4), core)
        return rcopy(tab.at[mine], tab.at[mine], gsend.at[which, late, k], grecv.at[which, late, mine], (n, to))

    def gain_a_wait(which, late):
        _, tab = table(which, late)
        for k in (1, 2, 3):
            o = lax.rem((y, x)[which] + k, 4)
            rcopy(tab.at[o], tab.at[o], gsend.at[which, late, k], grecv.at[which, late, o], (n, me)).wait_recv()

    def slot_dev(k, own):
        s = lax.rem(own + k, 8)
        return s, s // 2, lax.rem(s, 2)

    def bas_x(k):
        s, tx, tc = slot_dev(k, x * 2 + core)
        mine = x * 2 + core
        return rcopy(bx_v.at[mine], bx_v.at[mine], bsend.at[0, k], bxr.at[mine], (n, bl_of(y, tx, tc)))

    def bas_y(k):
        s, ty, tc = slot_dev(k, y * 2 + core)
        mine = y * 2 + core
        return rcopy(by_v.at[mine], by_v.at[mine], bsend.at[1, k], byr.at[mine], (n, bl_of(ty, x, tc)))

    for k in (1, 3, 2):
        for which in (0, 1):
            gain_a(which, 0, k).start()

    def start_bas(k):
        bas_x(k).start()
        bas_y(k).start()

    loop(8, start_bas, unroll=1, start=1)
    for k in (1, 3, 2):
        for which in (0, 1):
            gain_a(which, 1, k).start()
    early(1)
    start_early(1, 0)

    def meta(k):
        t = lax.rem(n + k, 4)
        return [
            rcopy(a, b, msend.at[i, k], mrecv.at[i, n], (t, me))
            for i, (a, b) in enumerate(
                (
                    (zflags.at[n], zflags.at[n]), (zoffs.at[n], zoffs.at[n]), (zw.at[n], zw.at[n]),
                    (zfirst.at[n], zfirst.at[n]),
                )
            )
        ]

    def wait_bas(k):
        sx = lax.rem(x * 2 + core + k, 8)
        sy = lax.rem(y * 2 + core + k, 8)
        rcopy(bx_v.at[sx], bx_v.at[sx], bsend.at[0, k], bxr.at[sx], (n, me)).wait_recv()
        rcopy(by_v.at[sy], by_v.at[sy], bsend.at[1, k], byr.at[sy], (n, me)).wait_recv()

    loop(8, wait_bas, unroll=1, start=1)
    to_s0 = pltpu.make_async_copy(bx_v, bx_s, local_sem.at[17])
    to_s1 = pltpu.make_async_copy(by_v, by_s, local_sem.at[18])
    to_s0.start()
    to_s1.start()
    gain_a_wait(0, 0)
    gain_a_wait(1, 0)
    to_s0.wait()
    to_s1.wait()

    slots = (lambda k: lax.rem(x * 2 + core + k, 8), lambda k: lax.rem(y * 2 + core + k, 8))
    asked_of = (bx_s, by_s)
    mine_of = (x * 2 + core, y * 2 + core)

    def pick(which, late, slot):
        out = ((m0, m1), (q0, q1))[late][which]
        _, tab = table(which, late)
        for r in range(ROWS):
            a = asked_of[which][slot, r // 4, r % 4]
            owner = lax.shift_right_logical(a * 5958, 16)
            at = a - owner * OWN_ANT
            ox, oy = (owner >> 1) & 3, owner >> 3
            fixed, moving, here = (ox, oy, x) if which == 0 else (oy, ox, y)
            w = flag((fixed == here) & ((owner & 1) == core))
            for p in range(2):
                out[slot, p, pl.ds(r, 1), :] = w * tab[moving, p, at]

    def gain_b(which, late, k):
        s, t, tc = slot_dev(k, mine_of[which])
        src = ((m0, m1), (q0, q1))[late][which]
        dst = ((c0, c1), (d0, d1))[late][which]
        to = bl_of(y, t, tc) if which == 0 else bl_of(t, x, tc)
        i = 2 * late + which
        return rcopy(src.at[s], dst.at[mine_of[which]], rsend.at[i, k], rrecv.at[i, mine_of[which]], (n, to))

    def send_rows(late):
        def go(k):
            for which in (0, 1):
                pick(which, late, slots[which](k))
                gain_b(which, late, k).start()

        loop(8, go, unroll=1, start=1)
        for which in (0, 1):
            pick(which, late, mine_of[which])
            dst = ((c0, c1), (d0, d1))[late][which]
            src = ((m0, m1), (q0, q1))[late][which]
            dst[mine_of[which]] = src[mine_of[which]]

    def gain_products(late):
        def wait(k):
            for which in (0, 1):
                s = slots[which](k)
                src = ((m0, m1), (q0, q1))[late][which]
                dst = ((c0, c1), (d0, d1))[late][which]
                i = 2 * late + which
                rcopy(src.at[s], dst.at[s], rsend.at[i, k], rrecv.at[i, s], (n, me)).wait_recv()

        loop(8, wait, unroll=1, start=1)
        for which in (0, 1):
            got = ((c0, c1), (d0, d1))[late][which]
            parts = []
            for p in range(2):
                acc = got[0, p]
                for s in range(1, 8):
                    acc = acc + got[s, p]
                parts.append(acc)
            A, B = parts
            cols = pl.ds(((512, 640), (0, 256))[late][which], LATER if late else SOON)
            G[0, :, cols] = A * swap4(A) + B * swap4(B)
            G[1, :, cols] = A * swap4(B) - B * swap4(A)

    send_rows(0)

    def pass_on(st):
        for h in (0, 1):
            for w in (0, 1):
                zcopy(st, w, h).wait_recv()
                forward(st, w, h).start()

    pass_on(0)
    start_early(1, 1)
    gain_a_wait(0, 1)
    gain_a_wait(1, 1)
    send_rows(1)
    for k in (1, 3, 2):
        for c in meta(k):
            c.start()

    samples(2)
    rate2 = phases(2)

    def last(e):
        Y[2, e] = turned(2, rate2, e)

    loop(BINS, last)
    gain_products(0)

    def bin_copy(st, t):
        if st >= 2:
            src = Y.at[2, t, :, pl.ds((st - 2) * HALF, HALF)]
            return rcopy(src, Y2.at[st - 2, me], asend.at[st], arecv.at[st], (n, t))
        return rcopy(S.at[st, t], landed.at[st, me], asend.at[st], arecv.at[st], (n, t))

    def all_bins(st):
        part = pl.ds(0, DEVS - 1)
        if st >= 2:
            return rcopy(Y2.at[st - 2, part], Y2.at[st - 2, part], asend.at[st], arecv.at[st], (n, me))
        return rcopy(S.at[st, part], landed.at[st, part], asend.at[st], arecv.at[st], (n, me))

    low_early = lax.broadcasted_iota(I32, (ROWS, EARLY), 0) < 4

    def gz(k):
        return rcopy(GP.at[n], GP.at[n], gzs.at[k], gzr.at[n], (lax.rem(n + k, 4), me))

    def share_gains():
        gain_products(1)
        GP[n] = jnp.where(low_early, G[0, :, pl.ds(0, EARLY)], G[1, :, pl.ds(0, EARLY)])
        for k in (2, 1, 3):
            gz(k).start()

    for g in (0, 1):
        cols = pl.ds(EARLY + g * HALF, HALF)
        gr, gs = G[0, :, cols], G[1, :, cols]
        part = pl.ds(g * HALF, HALF)

        def with_gain(t):
            v = Y[2, t, :, part]
            return gr * v + gs * swap4(v)

        def send_last(k):
            t = lax.rem(me + k, DEVS)
            Y[2, t, :, part] = with_gain(t)
            bin_copy(2 + g, t).start()

        loop(DEVS, send_last, unroll=1, start=1)
        Y2[g, me] = with_gain(me)
        if g == 0:
            share_gains()
    pass_on(1)

    for k in (1, 2, 3):
        o = lax.rem(n + k, 4)
        for i, (a, b) in enumerate(
            ((zflags.at[o], zflags.at[o]), (zoffs.at[o], zoffs.at[o]), (zw.at[o], zw.at[o]), (zfirst.at[o], zfirst.at[o]))
        ):
            rcopy(a, b, msend.at[i, k], mrecv.at[i, o], (n, me)).wait_recv()
    to_smem = [
        pltpu.make_async_copy(a, b, local_sem.at[19 + i])
        for i, (a, b) in enumerate(((zoffs, zoffs_s), (zw, zw_s), (zfirst, zfirst_s)))
    ]
    for c in to_smem:
        c.start()
    for c in to_smem:
        c.wait()
    first_down, first_up, first_far = zfirst_s[down, 0, 0], zfirst_s[up, 0, 0], zfirst_s[far, 0, 0]

    total = jnp.zeros((1, CH), F32)
    bin_here = n * BINS + me
    for k in range(NIGHTS):
        l = bin_here - zfirst_s[k, 0, 0]
        valid = flag((l >= 0) & (l < BINS))
        lc = jnp.clip(l, 0, BINS - 1)
        off = zoffs_s[k, 0, lc]
        for t in range(TAPS):
            bits = (zflags[k] >> (off + t)) & 1
            total = total + (valid * zw_s[k, t, lc]) * (1.0 - bits.astype(F32))
    wt_ref[...] = total
    scale = 1.0 / jnp.maximum(total, 0.5)

    def put(begin, k, a, b, inv):
        a, b = a * inv, b * inv
        low = lax.broadcasted_iota(I32, a.shape, 0) < 4
        at = pl.multiple_of(k * 8, 8)
        cols = pl.ds(begin, a.shape[1])
        out_ref[0, pl.ds(at, 8), cols] = jnp.where(low, a, swap4(b))
        out_ref[1, pl.ds(at, 8), cols] = jnp.where(low, swap4(a), b)

    def scale_of(st):
        return jnp.broadcast_to(scale[:, st * WIDE : (st + 1) * WIDE], (ROWS, WIDE))

    def last_first(g):
        all_bins(2 + g).wait_recv()
        s = shift_of(first, n, me)
        loop(HB, lambda j: first_message(2, g * HB + j, s, Y2[g, j], Y2[g, HB + j]))
        zcopy(2, 0, g).start()
        zcopy(2, 1, g).start()

    def last_second(g):
        zcopy(2, 0, g).wait_recv()
        zcopy(2, 1, g).wait_recv()
        loop(HB, lambda j: second_message(2, g * HB + j, me, Y2[g, j], Y2[g, HB + j]))
        zcopy(2, 2, g).start()
        zcopy(2, 3, g).start()

    last_first(0)

    for k in (1, 2, 3):
        o = lax.rem(n + k, 4)
        rcopy(GP.at[o], GP.at[o], gzs.at[k], gzr.at[o], (n, me)).wait_recv()
    for k in range(NIGHTS):
        packed = GP[k]
        turned_over = swap4(packed)
        GZ[k, 0] = jnp.where(low_early, packed, turned_over)
        GZ[k, 1] = jnp.where(low_early, -turned_over, packed)

    def combine(st, e):
        here = flag(shift_of(first, n, e) == 0)
        from_down = flag(shift_of(first_down, down, e) == 1)
        from_up = flag(shift_of(first_up, up, e) == 3)
        from_far = flag(shift_of(first_far, far, e) == 2)

        def part(half, terms):
            cols = pl.ds(st * WIDE + half * HALF, HALF)
            acc = None
            for night, v in terms:
                w = GZ[night, 0, :, cols] * v + GZ[night, 1, :, cols] * swap4(v)
                acc = w if acc is None else acc + w
            return acc

        a = part(
            0,
            (
                (n, here * Y[st, e, :, lo]), (up, from_up * r1n[st, e]), (down, r2p[st, e]),
                (far, from_far * r3p[st, e]),
            ),
        )
        b = part(
            1,
            (
                (n, here * Y[st, e, :, hi]), (down, from_down * r1p[st, e]), (up, r2n[st, e]),
                (far, from_far * r3n[st, e]),
            ),
        )
        return a, b

    def finish_early(st):
        for h in (0, 1):
            zcopy(st, 2, h).wait_recv()
            zcopy(st, 3, h).wait_recv()
            forward(st, 0, h).wait_recv()
            forward(st, 1, h).wait_recv()

        def go(k):
            t = lax.rem(me + k, DEVS)
            a, b = combine(st, t)
            S[st, t, :, lo] = a
            S[st, t, :, hi] = b
            bin_copy(st, t).start()

        loop(DEVS, go, unroll=1, start=1)
        a, b = combine(st, me)
        landed[st, me, :, lo] = a
        landed[st, me, :, hi] = b

    finish_early(0)
    last_first(1)
    finish_early(1)
    last_second(0)
    last_second(1)

    def assemble(st):
        all_bins(st).wait_recv()
        inv = scale_of(st)
        loop(DEVS // 2, lambda k: put(st * WIDE, k, landed[st, 2 * k], landed[st, 2 * k + 1], inv))

    assemble(0)
    here2 = flag(shift_of(first, n, me) == 0)
    down2 = flag(shift_of(first_down, down, me) == 1)
    up2 = flag(shift_of(first_up, up, me) == 3)
    for g in (0, 1):
        zcopy(2, 2, g).wait_recv()
        zcopy(2, 3, g).wait_recv()
        inv2 = scale_of(2)[:, g * HALF : (g + 1) * HALF]

        def finish(k):
            lower = [
                here2 * Y2[g, j] + up2 * r1n[2, g * HB + j] + r2p[2, g * HB + j] for j in (2 * k, 2 * k + 1)
            ]
            upper = [
                here2 * Y2[g, HB + j] + down2 * r1p[2, g * HB + j] + r2n[2, g * HB + j] for j in (2 * k, 2 * k + 1)
            ]
            put(EARLY + g * HALF, k, *lower, inv2)
            put(EARLY + g * HALF, HB // 2 + k, *upper, inv2)

        loop(HB // 2, finish)
    assemble(1)

    for k in (1, 2, 3):
        for which in (0, 1):
            for late in (0, 1):
                gain_a(which, late, k).wait_send()
        for c in meta(k):
            c.wait_send()
        gz(k).wait_send()

    def done(k):
        bas_x(k).wait_send()
        bas_y(k).wait_send()
        for which in (0, 1):
            for late in (0, 1):
                gain_b(which, late, k).wait_send()

    loop(8, done, unroll=1, start=1)
    for h in (0, 1):
        for st in range(STAGES):
            for w in range(4):
                zcopy(st, w, h).wait_send()
        for w in (0, 1):
            for st in (0, 1):
                forward(st, w, h).wait_send()
    for st in range(STAGES + 1):
        all_bins(st).wait_send()


def place_kernel(binned, wt, out, wt_out, sems):
    copies = [
        pltpu.make_async_copy(binned.at[p, pl.ds(k * 64, 64)], out.at[p, pl.ds(k * 64, 64)], sems.at[2 * p + k])
        for p in range(2)
        for k in range(2)
    ]
    copies.append(pltpu.make_async_copy(wt, wt_out, sems.at[4]))
    for c in copies:
        c.start()
    for c in copies:
        c.wait()


def per_device(
    visibilities, corrupted_sample_markers, antenna_gain_table, baseline_antennas, first_bin, tap_offsets, tap_weights,
    lst_delay, fringe_rate,
):
    vis = jnp.transpose(visibilities[:, 0], (0, 2, 1, 3))
    gains = jnp.transpose(antenna_gain_table, (0, 2, 1, 3))
    weights = jnp.transpose(tap_weights[0], (1, 0))
    bas = jnp.transpose(baseline_antennas, (1, 0))

    def held(a):
        return pltpu.with_memory_space_constraint(a, pltpu.HBM)

    vm = pl.BlockSpec(memory_space=pltpu.VMEM)
    hbm = pl.BlockSpec(memory_space=pltpu.HBM)
    D = pltpu.SemaphoreType.DMA
    msg = (STAGES, BINS, ROWS, HALF)
    binned, weight_total = pl.pallas_call(
        comm_kernel,
        out_shape=(
            pltpu.VMEM((2, 4 * DEVS, CH), F32),
            pltpu.VMEM((1, CH), F32),
        ),
        in_specs=[hbm] * 9,
        out_specs=(vm, vm),
        scratch_shapes=[
            pltpu.SMEM((1, BINS), I32),
            pltpu.SMEM((1,), I32),
            pltpu.SMEM((TAPS, BINS), F32),
            pltpu.SMEM((1, BINS), F32),
            pltpu.SMEM((4,), F32),
            pltpu.VMEM((2, SAMPLES, 4, CH), F32),
            pltpu.VMEM((SAMPLES, ROWS, CH), F32),
            pltpu.VMEM((STAGES, BINS, ROWS, WIDE), F32),
            pltpu.VMEM((2, DEVS, ROWS, HALF), F32),
            pltpu.VMEM((2, BINS, ROWS, WIDE), F32),
            pltpu.VMEM((2, DEVS, ROWS, WIDE), F32),
            *([pltpu.VMEM((4, 2, OWN_ANT, 1, SOON), F32)] * 2),
            *([pltpu.VMEM((4, 2, OWN_ANT, 1, LATER), F32)] * 2),
            pltpu.VMEM((8, 2, 4), I32),
            pltpu.VMEM((8, 2, 4), I32),
            pltpu.SMEM((8, 2, 4), I32),
            pltpu.SMEM((8, 2, 4), I32),
            *([pltpu.VMEM((8, 2, ROWS, SOON), F32)] * 4),
            *([pltpu.VMEM((8, 2, ROWS, LATER), F32)] * 4),
            pltpu.VMEM((2, ROWS, CH), F32),
            pltpu.VMEM((NIGHTS, ROWS, EARLY), F32),
            pltpu.VMEM((NIGHTS, 2, ROWS, EARLY), F32),
            pltpu.VMEM((NIGHTS, 1, CH), I32),
            pltpu.VMEM((NIGHTS, 1, HALF), I32),
            pltpu.VMEM((NIGHTS, 1, BINS), I32),
            pltpu.VMEM((NIGHTS, TAPS, BINS), F32),
            pltpu.SMEM((NIGHTS, 1, HALF), I32),
            pltpu.SMEM((NIGHTS, 1, BINS), I32),
            pltpu.SMEM((NIGHTS, TAPS, BINS), F32),
        ]
        + [pltpu.VMEM(msg, F32)] * 8
        + [pltpu.VMEM((2,) + msg[1:], F32)] * 2
        + [
            D((22,)), D((2, 2, 4)), D((2, 2, 4)), D((2, 8)), D((8,)), D((8,)), D((4, 4)), D((4, 4)),
            D((4, 8)), D((4, 8)), D((STAGES + 2, 4, 2)), D((STAGES + 2, 4, 2)), D((4,)), D((4,)),
            D((STAGES + 1,)), D((STAGES + 1,)),
        ],
        compiler_params=pltpu.CompilerParams(
            collective_id=0, has_side_effects=True, vmem_limit_bytes=48 * 1024 * 1024
        ),
        name="exchange",
    )(
        held(vis), held(gains), held(corrupted_sample_markers), held(tap_offsets), first_bin, held(weights),
        held(lst_delay), held(bas), held(fringe_rate),
    )
    binned, weight_total = pl.pallas_call(
        place_kernel,
        out_shape=(jax.ShapeDtypeStruct((2, 4 * DEVS, CH), F32), jax.ShapeDtypeStruct((1, CH), F32)),
        in_specs=[vm, vm],
        out_specs=(hbm, hbm),
        scratch_shapes=[D((5,))],
        compiler_params=pltpu.CompilerParams(vmem_limit_bytes=8 * 1024 * 1024),
        name="place",
    )(binned, weight_total)
    return binned.reshape(2, 1, 4 * DEVS, CH), weight_total


def solution(mesh):
    placed = (
        P(None, "night", "bl", None, None),
        P("night", None),
        P(None, "night", "bl", None),
        P("bl", None),
        P("night"),
        P("night", None),
        P("night", None, None),
        P("night", None),
        P("bl"),
    )
    return jax.shard_map(
        per_device,
        mesh=mesh,
        in_specs=placed,
        out_specs=(P(None, ("night", "bl"), None, None), P(("night", "bl"), None)),
        check_vma=False,
    )
```

time: 131 us -> 39.5 us (0.30)
  blocking collectives: 44.7 us -> 0 us
  waiting for transfers between devices: 39.9 us -> 0 us
  Pallas kernels: 0 us -> 38.1 us
  between operations: 14.8 us -> 1.29 us
  local copies, waits for them, and re-layouts: 13.3 us -> 0 us
  other arithmetic: 7.97 us -> 0 us
  starting transfers between devices: 7.14 us -> 0 us
  matrix products: 2.21 us -> 0 us
    pallas_call x0 -> x2, Pallas kernels: none -> 38.1 us  [the longest x1 37.2 us: per_device(): pl.pallas_call(comm_kernel, out_shape=(pltpu.VMEM((2, 4 * DEVS, CH), F32)...]
    all_gather x3 -> x0, blocking collectives: 28.1 us -> none  [the longest x1 11.1 us: per_device(): lax.all_gather(corrupted_sample_markers, 'night', axis=0, tiled=True)]
    all_to_all x1 -> x0, waiting for transfers between devices: 22.1 us -> none  [per_device(): lax.all_to_all(bin_grid.reshape(2, sources, LB_DEV, block_rows, channels)...]
    all_gather x1 -> x0, waiting for transfers between devices: 17.8 us -> none  [per_device(): gains_all = lax.all_gather(antenna_gain_table, 'bl', axis=2, tiled=True)]
    unnamed x1 -> x0, blocking collectives: 16.6 us -> none
    all_to_all x1 -> x0, starting transfers between devices: 7.1 us -> none  [per_device(): lax.all_to_all(bin_grid.reshape(2, sources, LB_DEV, block_rows, channels)...]
    gather x2 -> x0, local copies, waits for them, and re-layouts: 4.38 us -> none  [the longest x1 2.19 us: per_device(): first_gain = jnp.take(gains_all[:, 0], baseline_antennas[:, 0], axis=1)]
    unnamed x9 -> x0, local copies, waits for them, and re-layouts: 3.84 us -> none
  transfers between devices with their start and end apart: 2 -> 0, of which waited for: 2 -> 0; matrix products, arithmetic and copies ran while one was open for 4% -> 0% of each run, Pallas kernels for 0% -> 0%
where the time goes in v4:
time: 39.5 us; the launch traced here: 39.4 us
  Pallas kernels  38.1 us (96%)
  between operations  1.29 us (3%)
    pallas_call x1, Pallas kernels, per_device(): pl.pallas_call(comm_kernel, out_shape=(pltpu.VMEM((2, 4 * DEVS, CH), F32)...  37.2 us
    pallas_call x1, Pallas kernels, per_device(): pl.pallas_call(place_kernel, out_shape=(jax.ShapeDtypeStruct((2, 4 * DEVS...  0.92 us

profile of v4, /device:TPU:1, one launch (start us, length us, event | category | flops | bytes accessed | tf_op | source)
XLA Modules:
  0.0 39.4 jit_solution(4452058498626961706)
XLA Ops:
  1.3 37.2 %exchange.1 = (f32[2,128,768]{2,1,0:T(8,128)S(1)}, f32[1,768]{1,0:T(1,128)S(1)}) custom-call(f32[2,30,4,768]{3,2,1,0:T(4,128)} %bitcast.11, f32[2,11,1,768]{3,2,1,0:T(1,128)} %bitcast.12, s32[1,768]{1,0:T(1,128)} %flags_h.1, s32[1,32]{1,0:T(1,128)} %offs_h.1, s32[1]{0:T(128)S(6)} %copy.12.first_h, f32[4,32]{1,0:T(4,128)} %bitcast.13, f32[1,32]{1,0:T(1,128)} %delay_h.1, ...), custom_call_target="tpu_custom_call" | custom-call | tf_op jit(solution)/shard_map/exchange/pallas_call | solution.py:638
  38.5 0.9 %place.1 = (f32[2,128,768]{2,1,0:T(8,128)}, f32[1,768]{1,0:T(1,128)}) custom-call(f32[2,128,768]{2,1,0:T(8,128)S(1)} %get-tuple-element.6.binned, f32[1,768]{1,0:T(1,128)S(1)} %get-tuple-element.7.wt), custom_call_target="tpu_custom_call" | custom-call | tf_op jit(solution)/shard_map/place/pallas_call | solution.py:692

commit v5 on v4

--- a/solution.py
+++ b/solution.py
@@ -268,11 +268,6 @@
         bas_y(k).start()
 
     loop(8, start_bas, unroll=1, start=1)
-    for k in (1, 3, 2):
-        for which in (0, 1):
-            gain_a(which, 1, k).start()
-    early(1)
-    start_early(1, 0)
 
     def meta(k):
         t = lax.rem(n + k, 4)
@@ -285,6 +280,24 @@
                 )
             )
         ]
+
+    for k in (1, 3, 2):
+        for c in meta(k):
+            c.start()
+    for k in (1, 3, 2):
+        for which in (0, 1):
+            gain_a(which, 1, k).start()
+    early(1)
+    start_early(1, 0)
+
+    def pass_on(st):
+        for h in (0, 1):
+            for w in (0, 1):
+                zcopy(st, w, h).wait_recv()
+                forward(st, w, h).start()
+
+    pass_on(0)
+    start_early(1, 1)
 
     def wait_bas(k):
         sx = lax.rem(x * 2 + core + k, 8)
@@ -365,20 +378,9 @@
 
     send_rows(0)
 
-    def pass_on(st):
-        for h in (0, 1):
-            for w in (0, 1):
-                zcopy(st, w, h).wait_recv()
-                forward(st, w, h).start()
-
-    pass_on(0)
-    start_early(1, 1)
     gain_a_wait(0, 1)
     gain_a_wait(1, 1)
     send_rows(1)
-    for k in (1, 3, 2):
-        for c in meta(k):
-            c.start()
 
     samples(2)
     rate2 = phases(2)
@@ -406,6 +408,21 @@
     def gz(k):
         return rcopy(GP.at[n], GP.at[n], gzs.at[k], gzr.at[n], (lax.rem(n + k, 4), me))
 
+    def load_meta():
+        for k in (1, 2, 3):
+            o = lax.rem(n + k, 4)
+            for i, (a, b) in enumerate(
+                ((zflags.at[o], zflags.at[o]), (zoffs.at[o], zoffs.at[o]), (zw.at[o], zw.at[o]), (zfirst.at[o], zfirst.at[o]))
+            ):
+                rcopy(a, b, msend.at[i, k], mrecv.at[i, o], (n, me)).wait_recv()
+        to_smem = [
+            pltpu.make_async_copy(a, b, local_sem.at[19 + i])
+            for i, (a, b) in enumerate(((zoffs, zoffs_s), (zw, zw_s), (zfirst, zfirst_s)))
+        ]
+        for c in to_smem:
+            c.start()
+        return to_smem
+
     def share_gains():
         gain_products(1)
         GP[n] = jnp.where(low_early, G[0, :, pl.ds(0, EARLY)], G[1, :, pl.ds(0, EARLY)])
@@ -430,20 +447,9 @@
         Y2[g, me] = with_gain(me)
         if g == 0:
             share_gains()
+            to_smem = load_meta()
     pass_on(1)
 
-    for k in (1, 2, 3):
-        o = lax.rem(n + k, 4)
-        for i, (a, b) in enumerate(
-            ((zflags.at[o], zflags.at[o]), (zoffs.at[o], zoffs.at[o]), (zw.at[o], zw.at[o]), (zfirst.at[o], zfirst.at[o]))
-        ):
-            rcopy(a, b, msend.at[i, k], mrecv.at[i, o], (n, me)).wait_recv()
-    to_smem = [
-        pltpu.make_async_copy(a, b, local_sem.at[19 + i])
-        for i, (a, b) in enumerate(((zoffs, zoffs_s), (zw, zw_s), (zfirst, zfirst_s)))
-    ]
-    for c in to_smem:
-        c.start()
     for c in to_smem:
         c.wait()
     first_down, first_up, first_far = zfirst_s[down, 0, 0], zfirst_s[up, 0, 0], zfirst_s[far, 0, 0]
@@ -486,16 +492,15 @@
         zcopy(2, 2, g).start()
         zcopy(2, 3, g).start()
 
-    last_first(0)
-
-    for k in (1, 2, 3):
-        o = lax.rem(n + k, 4)
-        rcopy(GP.at[o], GP.at[o], gzs.at[k], gzr.at[o], (n, me)).wait_recv()
-    for k in range(NIGHTS):
-        packed = GP[k]
-        turned_over = swap4(packed)
-        GZ[k, 0] = jnp.where(low_early, packed, turned_over)
-        GZ[k, 1] = jnp.where(low_early, -turned_over, packed)
+    def unpack_gains():
+        for k in (1, 2, 3):
+            o = lax.rem(n + k, 4)
+            rcopy(GP.at[o], GP.at[o], gzs.at[k], gzr.at[o], (n, me)).wait_recv()
+        for k in range(NIGHTS):
+            packed = GP[k]
+            turned_over = swap4(packed)
+            GZ[k, 0] = jnp.where(low_early, packed, turned_over)
+            GZ[k, 1] = jnp.where(low_early, -turned_over, packed)
 
     def combine(st, e):
         here = flag(shift_of(first, n, e) == 0)
@@ -546,6 +551,8 @@
         landed[st, me, :, lo] = a
         landed[st, me, :, hi] = b
 
+    last_first(0)
+    unpack_gains()
     finish_early(0)
     last_first(1)
     finish_early(1)

time: 39.5 us -> 39 us (0.987)
  Pallas kernels: 38.1 us -> 37.6 us
    pallas_call x1, Pallas kernels: 37.2 us -> 36.6 us  [per_device(): pl.pallas_call(comm_kernel, out_shape=(pltpu.VMEM((2, 4 * DEVS, CH), F32)...]
where the time goes in v5:
time: 39 us; the launch traced here: 38.9 us
  Pallas kernels  37.6 us (96%)
  between operations  1.29 us (3%)
    pallas_call x1, Pallas kernels, per_device(): pl.pallas_call(comm_kernel, out_shape=(pltpu.VMEM((2, 4 * DEVS, CH), F32)...  36.6 us
    pallas_call x1, Pallas kernels, per_device(): pl.pallas_call(place_kernel, out_shape=(jax.ShapeDtypeStruct((2, 4 * DEVS...  0.92 us

profile of v5, /device:TPU:1, one launch (start us, length us, event | category | flops | bytes accessed | tf_op | source)
XLA Modules:
  0.0 38.9 jit_solution(6961963373496065725)
XLA Ops:
  1.3 36.6 %exchange.1 = (f32[2,128,768]{2,1,0:T(8,128)S(1)}, f32[1,768]{1,0:T(1,128)S(1)}) custom-call(f32[2,30,4,768]{3,2,1,0:T(4,128)} %bitcast.11, f32[2,11,1,768]{3,2,1,0:T(1,128)} %bitcast.12, s32[1,768]{1,0:T(1,128)} %flags_h.1, s32[1,32]{1,0:T(1,128)} %offs_h.1, s32[1]{0:T(128)S(6)} %copy.12.first_h, f32[4,32]{1,0:T(4,128)} %bitcast.13, f32[1,32]{1,0:T(1,128)} %delay_h.1, ...), custom_call_target="tpu_custom_call" | custom-call | tf_op jit(solution)/shard_map/exchange/pallas_call | solution.py:645
  37.9 0.9 %place.1 = (f32[2,128,768]{2,1,0:T(8,128)}, f32[1,768]{1,0:T(1,128)}) custom-call(f32[2,128,768]{2,1,0:T(8,128)S(1)} %get-tuple-element.6.binned, f32[1,768]{1,0:T(1,128)S(1)} %get-tuple-element.7.wt), custom_call_target="tpu_custom_call" | custom-call | tf_op jit(solution)/shard_map/place/pallas_call | solution.py:699

commit v6 on v5

--- a/solution.py
+++ b/solution.py
@@ -443,7 +443,8 @@
             Y[2, t, :, part] = with_gain(t)
             bin_copy(2 + g, t).start()
 
-        loop(DEVS, send_last, unroll=1, start=1)
+        loop(29, send_last, unroll=4, start=1)
+        loop(DEVS, send_last, unroll=3, start=29)
         Y2[g, me] = with_gain(me)
         if g == 0:
             share_gains()
@@ -546,7 +547,8 @@
             S[st, t, :, hi] = b
             bin_copy(st, t).start()
 
-        loop(DEVS, go, unroll=1, start=1)
+        loop(29, go, unroll=4, start=1)
+        loop(DEVS, go, unroll=3, start=29)
         a, b = combine(st, me)
         landed[st, me, :, lo] = a
         landed[st, me, :, hi] = b
@@ -565,6 +567,33 @@
         loop(DEVS // 2, lambda k: put(st * WIDE, k, landed[st, 2 * k], landed[st, 2 * k + 1], inv))
 
     assemble(0)
+
+    for k in (1, 2, 3):
+        for which in (0, 1):
+            for late in (0, 1):
+                gain_a(which, late, k).wait_send()
+        for c in meta(k):
+            c.wait_send()
+        gz(k).wait_send()
+
+    def done(k):
+        bas_x(k).wait_send()
+        bas_y(k).wait_send()
+        for which in (0, 1):
+            for late in (0, 1):
+                gain_b(which, late, k).wait_send()
+
+    loop(8, done, unroll=1, start=1)
+    for h in (0, 1):
+        for st in range(STAGES):
+            for w in range(4 if st < 2 else 2):
+                zcopy(st, w, h).wait_send()
+        for w in (0, 1):
+            for st in (0, 1):
+                forward(st, w, h).wait_send()
+    for st in (0, 2, 3):
+        all_bins(st).wait_send()
+
     here2 = flag(shift_of(first, n, me) == 0)
     down2 = flag(shift_of(first_down, down, me) == 1)
     up2 = flag(shift_of(first_up, up, me) == 3)
@@ -585,32 +614,10 @@
 
         loop(HB // 2, finish)
     assemble(1)
-
-    for k in (1, 2, 3):
-        for which in (0, 1):
-            for late in (0, 1):
-                gain_a(which, late, k).wait_send()
-        for c in meta(k):
-            c.wait_send()
-        gz(k).wait_send()
-
-    def done(k):
-        bas_x(k).wait_send()
-        bas_y(k).wait_send()
-        for which in (0, 1):
-            for late in (0, 1):
-                gain_b(which, late, k).wait_send()
-
-    loop(8, done, unroll=1, start=1)
     for h in (0, 1):
-        for st in range(STAGES):
-            for w in range(4):
-                zcopy(st, w, h).wait_send()
-        for w in (0, 1):
-            for st in (0, 1):
-                forward(st, w, h).wait_send()
-    for st in range(STAGES + 1):
-        all_bins(st).wait_send()
+        zcopy(2, 2, h).wait_send()
+        zcopy(2, 3, h).wait_send()
+    all_bins(1).wait_send()
 
 
 def place_kernel(binned, wt, out, wt_out, sems):

time: 39 us -> 38.8 us (level)
  no operation moved by 1% of the time
where the time goes in v6:
time: 38.8 us; the launch traced here: 38.7 us
  Pallas kernels  37.4 us (96%)
  between operations  1.29 us (3%)
    pallas_call x1, Pallas kernels, per_device(): pl.pallas_call(comm_kernel, out_shape=(pltpu.VMEM((2, 4 * DEVS, CH), F32)...  36.5 us
    pallas_call x1, Pallas kernels, per_device(): pl.pallas_call(place_kernel, out_shape=(jax.ShapeDtypeStruct((2, 4 * DEVS...  0.92 us

profile of v6, /device:TPU:1, one launch (start us, length us, event | category | flops | bytes accessed | tf_op | source)
XLA Modules:
  0.0 38.7 jit_solution(3326628387619562602)
XLA Ops:
  1.3 36.5 %exchange.1 = (f32[2,128,768]{2,1,0:T(8,128)S(1)}, f32[1,768]{1,0:T(1,128)S(1)}) custom-call(f32[2,30,4,768]{3,2,1,0:T(4,128)} %bitcast.11, f32[2,11,1,768]{3,2,1,0:T(1,128)} %bitcast.12, s32[1,768]{1,0:T(1,128)} %flags_h.1, s32[1,32]{1,0:T(1,128)} %offs_h.1, s32[1]{0:T(128)S(6)} %copy.12.first_h, f32[4,32]{1,0:T(4,128)} %bitcast.13, f32[1,32]{1,0:T(1,128)} %delay_h.1, ...), custom_call_target="tpu_custom_call" | custom-call | tf_op jit(solution)/shard_map/exchange/pallas_call | solution.py:652
  37.8 0.9 %place.1 = (f32[2,128,768]{2,1,0:T(8,128)}, f32[1,768]{1,0:T(1,128)}) custom-call(f32[2,128,768]{2,1,0:T(8,128)S(1)} %get-tuple-element.6.binned, f32[1,768]{1,0:T(1,128)S(1)} %get-tuple-element.7.wt), custom_call_target="tpu_custom_call" | custom-call | tf_op jit(solution)/shard_map/place/pallas_call | solution.py:706

commit v7 on v6

--- a/solution.py
+++ b/solution.py
@@ -622,11 +622,11 @@
 
 def place_kernel(binned, wt, out, wt_out, sems):
     copies = [
-        pltpu.make_async_copy(binned.at[p, pl.ds(k * 64, 64)], out.at[p, pl.ds(k * 64, 64)], sems.at[2 * p + k])
+        pltpu.make_async_copy(binned.at[p, pl.ds(k * 16, 16)], out.at[p, pl.ds(k * 16, 16)], sems.at[8 * p + k])
         for p in range(2)
-        for k in range(2)
+        for k in range(8)
     ]
-    copies.append(pltpu.make_async_copy(wt, wt_out, sems.at[4]))
+    copies.append(pltpu.make_async_copy(wt, wt_out, sems.at[16]))
     for c in copies:
         c.start()
     for c in copies:
@@ -708,7 +708,7 @@
         out_shape=(jax.ShapeDtypeStruct((2, 4 * DEVS, CH), F32), jax.ShapeDtypeStruct((1, CH), F32)),
         in_specs=[vm, vm],
         out_specs=(hbm, hbm),
-        scratch_shapes=[D((5,))],
+        scratch_shapes=[D((17,))],
         compiler_params=pltpu.CompilerParams(vmem_limit_bytes=8 * 1024 * 1024),
         name="place",
     )(binned, weight_total)

time: 38.8 us -> 38.9 us (level)
  no operation moved by 1% of the time
where the time goes in v7:
time: 38.9 us; the launch traced here: 38.8 us
  Pallas kernels  37.5 us (96%)
  between operations  1.29 us (3%)
    pallas_call x1, Pallas kernels, per_device(): pl.pallas_call(comm_kernel, out_shape=(pltpu.VMEM((2, 4 * DEVS, CH), F32)...  36.5 us
    pallas_call x1, Pallas kernels, per_device(): pl.pallas_call(place_kernel, out_shape=(jax.ShapeDtypeStruct((2, 4 * DEVS...  1.01 us

profile of v7, /device:TPU:1, one launch (start us, length us, event | category | flops | bytes accessed | tf_op | source)
XLA Modules:
  0.0 38.8 jit_solution(1589196027935282173)
XLA Ops:
  1.3 36.5 %exchange.1 = (f32[2,128,768]{2,1,0:T(8,128)S(1)}, f32[1,768]{1,0:T(1,128)S(1)}) custom-call(f32[2,30,4,768]{3,2,1,0:T(4,128)} %bitcast.11, f32[2,11,1,768]{3,2,1,0:T(1,128)} %bitcast.12, s32[1,768]{1,0:T(1,128)} %flags_h.1, s32[1,32]{1,0:T(1,128)} %offs_h.1, s32[1]{0:T(128)S(6)} %copy.12.first_h, f32[4,32]{1,0:T(4,128)} %bitcast.13, f32[1,32]{1,0:T(1,128)} %delay_h.1, ...), custom_call_target="tpu_custom_call" | custom-call | tf_op jit(solution)/shard_map/exchange/pallas_call | solution.py:652
  37.8 1.0 %place.1 = (f32[2,128,768]{2,1,0:T(8,128)}, f32[1,768]{1,0:T(1,128)}) custom-call(f32[2,128,768]{2,1,0:T(8,128)S(1)} %get-tuple-element.6.binned, f32[1,768]{1,0:T(1,128)S(1)} %get-tuple-element.7.wt), custom_call_target="tpu_custom_call" | custom-call | tf_op jit(solution)/shard_map/place/pallas_call | solution.py:706

commit v8 on v7

--- a/solution.py
+++ b/solution.py
@@ -296,8 +296,8 @@
                 zcopy(st, w, h).wait_recv()
                 forward(st, w, h).start()
 
+    start_early(1, 1)
     pass_on(0)
-    start_early(1, 1)
 
     def wait_bas(k):
         sx = lax.rem(x * 2 + core + k, 8)

time: 38.9 us -> 38.9 us (level)
  no operation moved by 1% of the time
where the time goes in v8:
time: 38.9 us; the launch traced here: 38.8 us
  Pallas kernels  37.5 us (96%)
  between operations  1.29 us (3%)
    pallas_call x1, Pallas kernels, per_device(): pl.pallas_call(comm_kernel, out_shape=(pltpu.VMEM((2, 4 * DEVS, CH), F32)...  36.5 us
    pallas_call x1, Pallas kernels, per_device(): pl.pallas_call(place_kernel, out_shape=(jax.ShapeDtypeStruct((2, 4 * DEVS...  1.01 us

profile of v8, /device:TPU:1, one launch (start us, length us, event | category | flops | bytes accessed | tf_op | source)
XLA Modules:
  0.0 38.8 jit_solution(17444226814912145885)
XLA Ops:
  1.3 36.5 %exchange.1 = (f32[2,128,768]{2,1,0:T(8,128)S(1)}, f32[1,768]{1,0:T(1,128)S(1)}) custom-call(f32[2,30,4,768]{3,2,1,0:T(4,128)} %bitcast.11, f32[2,11,1,768]{3,2,1,0:T(1,128)} %bitcast.12, s32[1,768]{1,0:T(1,128)} %flags_h.1, s32[1,32]{1,0:T(1,128)} %offs_h.1, s32[1]{0:T(128)S(6)} %copy.12.first_h, f32[4,32]{1,0:T(4,128)} %bitcast.13, f32[1,32]{1,0:T(1,128)} %delay_h.1, ...), custom_call_target="tpu_custom_call" | custom-call | tf_op jit(solution)/shard_map/exchange/pallas_call | solution.py:652
  37.8 1.0 %place.1 = (f32[2,128,768]{2,1,0:T(8,128)}, f32[1,768]{1,0:T(1,128)}) custom-call(f32[2,128,768]{2,1,0:T(8,128)S(1)} %get-tuple-element.6.binned, f32[1,768]{1,0:T(1,128)S(1)} %get-tuple-element.7.wt), custom_call_target="tpu_custom_call" | custom-call | tf_op jit(solution)/shard_map/place/pallas_call | solution.py:706
